TPU v7x, 512 devices: a whole 4x4x16 slice. The times are simulated.
512 devices in a mesh: gx: 8 (over z_hi, y), gy: 8 (over x, core), gz: 8 (over z_lo).
Axes of the slice: x: 4, y: 4, z: 16 (z_hi: 2, z_lo: 8; z = z_hi * 8 + z_lo), core: 2. Of those that a mesh axis runs over, the one named last changes fastest.
Arguments:
- species: float32 [512, 512, 1024], P('gx', 'gz', 'gy'), may hold values from -6 to 6
- factor_y: float32 [1024, 96], P('gy'), may hold values from -0.1875 to 0.1875
- factor_z: float32 [512, 96], P('gz'), may hold values from -0.25 to 0.25
Outputs:
- gram: float32 [512, 512], P('gx', ('gy', 'gz'))
All inputs are finite; a program needn't handle non-finite values.
Results may differ from a plain program's by a relative error of at most 0.000062.
Values sent between devices are 32-bit elements; how exact they have to be, the bound alone decides.
No kernel may reach another device: no remote copies, remote signals or barrier semaphores. Data moves between devices by JAX's collectives and lax.ppermute only.
A program may use at most 64 MiB of HBM per device.

v0:
```python
import jax
import jax.numpy as jnp
from jax import lax
from jax.sharding import PartitionSpec as P

R = 96


def body(species, factor_y, factor_z):
    high = lax.Precision.HIGHEST
    along_y = jnp.einsum("xzy,yr->xzr", species, factor_y, precision=high)
    along_y = lax.psum_scatter(along_y, "gy", scatter_dimension=2, tiled=True)
    both = jnp.einsum("xzr,zs->xsr", along_y, factor_z, precision=high)
    block = lax.psum_scatter(both, "gz", scatter_dimension=1, tiled=True)
    own_rows = block.reshape(block.shape[0], -1)
    terms = jnp.dot(
        own_rows,
        lax.all_gather(own_rows, "gx", axis=0, tiled=True).T,
        precision=high,
        preferred_element_type=jnp.float32,
    )
    summed = lax.psum_scatter(terms, ("gy", "gz"), scatter_dimension=1, tiled=True)
    return summed / (R * R)


def solution(mesh):
    placed = (P("gx", "gz", "gy"), P("gy", None), P("gz", None))
    return jax.shard_map(
        body, mesh=mesh, in_specs=placed, out_specs=P("gx", ("gy", "gz")), check_vma=False
    )
```

profile of v0, /device:TPU:1, one launch (start us, length us, event | category | flops | bytes accessed | tf_op | source)
XLA Modules:
  0.0 974.0 jit_solution(16858907381971135245)
XLA Ops:
  6.5 0.0 copy-start
  6.5 0.0 reduce-scatter.3.cloned.1.call-start
  6.5 1.6 copy-done
  8.1 6.9 fusion
  15.1 3.5 copy.8
  18.6 0.0 copy-start.1
  18.6 0.0 reduce-scatter.3.cloned.1.call-update
  18.6 0.0 reduce-scatter.5.cloned.1.call-start
  18.6 46.8 %reduce-scatter.3.cloned.1.call-done = f32[64,64,12]{1,0,2:T(8,128)} async-done(((f32[64,64,96]{1,0,2:T(8,128)}), f32[64,64,12]{1,0,2:T(8,128)}) %reduce-scatter.3.cloned.1.call-update) | async-done | bytes 196624 | tf_op jit(solution)/shard_map/reduce_scatter | solution.py:12
  65.5 0.0 copy-done.1
  65.5 1.4 convolution_bitcast_fusion
  66.9 1.2 copy.9
  68.1 0.0 reduce-scatter.5.cloned.1.call-update
  68.2 0.0 all-reduce.3.cloned.1.call-start
  68.2 61.7 %reduce-scatter.5.cloned.1.call-done = f32[64,12,12]{0,2,1:T(8,128)} async-done(((f32[64,96,12]{0,2,1:T(8,128)}), f32[64,12,12]{0,2,1:T(8,128)}) %reduce-scatter.5.cloned.1.call-update) | async-done | bytes 36880 | tf_op jit(solution)/shard_map/reduce_scatter | solution.py:14
  129.9 0.9 reshape.3
  130.8 0.1 copy.10
  130.9 60.7 %all_gather.3 = f32[512,144]{1,0:T(8,128)S(1)} all-gather(f32[64,144]{1,0:T(8,128)S(1)} %copy.10), channel_id=1, replica_groups=mesh['gx'=8,'gy'=8,'gz'=8] {'gx'}, dimensions={0}, use_global_device_ids=true | all-gather | bytes 331776 | tf_op jit(solution)/shard_map/all_gather | solution.py:18
  191.6 1.3 fusion.3
  192.9 0.0 all-reduce.3.cloned.1.call-update
  192.9 1.3 dynamic-slice
  194.8 771.4 %all-reduce.3.cloned.1.call-done = f32[64,512]{0,1:T(8,128)} async-done(((f32[64,512]{0,1:T(8,128)}), f32[64,512]{0,1:T(8,128)}) %all-reduce.3.cloned.1.call-update) | async-done | bytes 131088
  966.2 1.3 dynamic-slice_multiply_fusion
Async XLA Ops:
  6.5 1.6 copy-start
  6.5 58.9 %reduce-scatter.3.cloned.1.call-start = ((), (), s32[]{:S(2)}) async-start(), calls=%async_computation.2 | async-start | bytes 3538944 | tf_op jit(solution)/shard_map/reduce_scatter | solution.py:12
  18.6 46.9 %copy-start.1 = (f32[64,96]{1,0:T(8,128)S(1)}, f32[64,96]{1,0:T(8,128)}, u32[]{:S(2)}) copy-start(f32[64,96]{1,0:T(8,128)} %param.5) | copy-start | bytes 73732
  18.6 111.3 %reduce-scatter.5.cloned.1.call-start = ((), (), s32[]{:S(2)}) async-start(), calls=%async_computation.3 | async-start | bytes 884736 | tf_op jit(solution)/shard_map/reduce_scatter | solution.py:14
  68.2 898.0 %all-reduce.3.cloned.1.call-start = ((), (), s32[]{:S(2)}) async-start(), calls=%async_computation.4 | async-start | bytes 524288
Sparse Core Ops, SparseCore 0:
  18.7 46.7 reduce-scatter.2
  68.3 61.5 reduce-scatter.4
  193.0 773.1 all-reduce.2
where the time goes:
time: 987 us; the launch traced here: 974 us
  waiting for transfers between devices  880 us (89%)
  blocking collectives  60.7 us (6%)
  between operations  13.8 us (1%)
    unnamed x4, waiting for transfers between devices  771 us
    reduce_scatter x1, waiting for transfers between devices, body(): block = lax.psum_scatter(both, 'gz', scatter_dimension=1, tiled=True)  61.7 us
    all_gather x1, blocking collectives, body(): lax.all_gather(own_rows, 'gx', axis=0, tiled=True)  60.7 us
    reduce_scatter x1, waiting for transfers between devices, body(): along_y = lax.psum_scatter(along_y, 'gy', scatter_dimension=2, tiled=True)  46.8 us
  transfers between devices with their start and end apart: 3, of which 3 were waited for; matrix products, arithmetic and copies ran while one was open for 0% of the time, Pallas kernels for 0%

commit v1 on v0

v1 whole, which is shorter than its diff:
```python
import jax
import jax.numpy as jnp
from jax import lax
from jax.sharding import Mesh, PartitionSpec as P

R = 96
HIGH = lax.Precision.HIGH


def body(species, factor_y, factor_z):
    y = lax.axis_index("y")
    x = lax.axis_index("x")
    c = lax.axis_index("c")
    all_z = lax.all_gather(factor_z, "g", axis=0, tiled=True)

    own = species.reshape(4, 16 * 64, 128)
    mine = lax.dynamic_slice(factor_y, (0, c * 48), (128, 48))
    others = lax.dynamic_slice(factor_y, (0, (1 - c) * 48), (128, 48))
    sent = jnp.einsum("jmy,yr->jrm", own, others, precision=HIGH)
    sent = lax.ppermute(sent, "c", [(0, 1), (1, 0)])
    along_y = jnp.einsum("jmy,yr->jrm", own, mine, precision=HIGH) + sent
    along_y = lax.all_to_all(along_y, "x", 0, 0, tiled=True).sum(0)

    parts = along_y.reshape(16, 24, 128)
    parts = lax.all_to_all(parts, ("h", "g"), 0, 0, tiled=True)
    parts = parts.reshape(2, 8, 3, 16, 64)
    both = jnp.einsum("hgixz,gzs->hixs", parts, all_z.reshape(8, 64, R), precision=HIGH)

    both = jnp.pad(both.reshape(96, R), ((0, 0), (0, 32)))
    both = lax.all_to_all(jnp.broadcast_to(both, (16, 96, 128)), ("y", "x"), 0, 0, tiled=True)
    both = both.reshape(4, 4, 2, 3, 16, 128)
    rows = lax.dynamic_index_in_dim(both, y, 0, keepdims=False)
    cols = lax.dynamic_slice(both, (2 * (x % 2), 0, x // 2, 0, 0, 0), (2, 4, 1, 3, 16, 128))[:, :, 0]
    terms = jnp.einsum("bjims,khins->bjmhkn", cols, rows, precision=HIGH)
    terms = terms.reshape(2, 8, 8, 2, 64).transpose(0, 3, 1, 2, 4).reshape(32, 4, 128)
    terms = lax.all_to_all(terms, ("c", "h", "g"), 0, 0, tiled=True).sum(0)
    return terms.reshape(8, 64).T / (R * R)


def solution(mesh):
    fine = Mesh(mesh.devices.reshape(2, 4, 4, 2, 8), ("h", "y", "x", "c", "g"))
    placed = (P(("h", "y"), "g", ("x", "c")), P(("x", "c"), None), P("g", None))
    return jax.shard_map(
        body, mesh=fine, in_specs=placed, out_specs=P(("h", "y"), ("x", "c", "g")), check_vma=False
    )
```

time: 987 us -> 140 us (0.14); the launches traced: 974 us -> 139 us
  waiting for transfers between devices: 880 us -> 12.4 us
  blocking collectives: 60.7 us -> 90.5 us
  starting transfers between devices: 0.09 us -> 24 us
  between operations: 13.8 us -> 0.15 us
    unnamed x4 -> x0, waiting for transfers between devices: 771 us -> none
    reduce_scatter x2 -> x0, waiting for transfers between devices: 108 us -> none  [the longest x1 61.7 us: body(): block = lax.psum_scatter(both, 'gz', scatter_dimension=1, tiled=True)]
    all_to_all x0 -> x2, blocking collectives: none -> 48.9 us  [the longest x1 34.5 us: body(): terms = lax.all_to_all(terms, ('c', 'h', 'g'), 0, 0, tiled=True).sum(0)]
    all_gather x1, blocking collectives: 60.7 us -> 41.6 us  [body(): all_z = lax.all_gather(factor_z, 'g', axis=0, tiled=True)]
    all_to_all x0 -> x2, starting transfers between devices: none -> 15.2 us  [the longest x1 10.3 us: body(): parts = lax.all_to_all(parts, ('h', 'g'), 0, 0, tiled=True)]
    all_to_all x0 -> x2, waiting for transfers between devices: none -> 10.4 us  [the longest x1 10.4 us: body(): lax.all_to_all(jnp.broadcast_to(both, (16, 96, 128)), ('y', 'x'), 0, 0, t...]
  transfers between devices with their start and end apart: 3 -> 3, of which waited for: 3 -> 2; matrix products, arithmetic and copies ran while one was open for 0% -> 0% of each run, Pallas kernels for 0% -> 0%
where the time goes in v1:
time: 140 us; the launch traced here: 139 us
  blocking collectives  90.5 us (65%)
  starting transfers between devices  24 us (17%)
  waiting for transfers between devices  12.4 us (9%)
  matrix products  6.23 us (4%)
  local copies, waits for them, and re-layouts  5.67 us (4%)
    all_gather x1, blocking collectives, body(): all_z = lax.all_gather(factor_z, 'g', axis=0, tiled=True)  41.6 us
    all_to_all x1, blocking collectives, body(): terms = lax.all_to_all(terms, ('c', 'h', 'g'), 0, 0, tiled=True).sum(0)  34.5 us
    all_to_all x1, blocking collectives, body(): along_y = lax.all_to_all(along_y, 'x', 0, 0, tiled=True).sum(0)  14.4 us
    all_to_all x1, waiting for transfers between devices, body(): lax.all_to_all(jnp.broadcast_to(both, (16, 96, 128)), ('y', 'x'), 0, 0, t...  10.4 us
    all_to_all x1, starting transfers between devices, body(): parts = lax.all_to_all(parts, ('h', 'g'), 0, 0, tiled=True)  10.3 us
    ppermute x1, starting transfers between devices, body(): sent = lax.ppermute(sent, 'c', [(0, 1), (1, 0)])  8.79 us
    all_to_all x1, starting transfers between devices, body(): lax.all_to_all(jnp.broadcast_to(both, (16, 96, 128)), ('y', 'x'), 0, 0, t...  4.89 us
  transfers between devices with their start and end apart: 3, of which 2 were waited for; matrix products, arithmetic and copies ran while one was open for 0% of the time, Pallas kernels for 0%

profile of v1, /device:TPU:1, one launch (start us, length us, event | category | flops | bytes accessed | tf_op | source)
XLA Modules:
  0.0 139.1 jit_solution(7124857604598433823)
XLA Ops:
  0.0 0.0 copy-start
  0.0 0.0 copy-start.2
  0.0 1.6 %copy-done = f32[64,64,128]{2,1,0:T(8,128)S(1)} copy-done((f32[64,64,128]{2,1,0:T(8,128)S(1)}, f32[64,64,128]{2,1,0:T(8,128)}, u32[]{:S(2)}) %copy-start) | copy-done | bytes 2097176
  1.6 1.9 %convolution_bitcast_fusion = f32[4,48,1024]{2,1,0:T(8,128)S(1)} fusion(f32[4,1024,128]{2,1,0:T(8,128)S(1)} %bitcast.48, f32[128,96]{0,1:T(8,128)} %param.4, s32[]{:T(128)S(6)} %select_n.28), kind=kOutput, calls=%fused_computation | convolution fusion | flops 150994944 | bytes 2908164 | tf_op jit(solution)/shard_map/jmy,yr->jrm/dot_general | solution.py:19
  3.5 8.8 %collective-permute-start = (f32[4,48,1024]{2,1,0:T(8,128)S(1)}, f32[4,48,1024]{2,1,0:T(8,128)}, u32[]{:S(2)}, u32[]{:S(2)}) collective-permute-start(f32[4,48,1024]{2,1,0:T(8,128)S(1)} %convolution_bitcast_fusion), channel_id=1, source_target_pairs={{0,8},{8,0},{1,9},{9,1},{2,10},{10,2},{3,11},{11,3},{4,12},{12,4},... | collective-permute-start | bytes 2359304 | tf_op jit(solution)/shard_map/ppermute | solution.py:20
  12.3 2.0 %collective-permute-done = f32[4,48,1024]{2,1,0:T(8,128)} collective-permute-done((f32[4,48,1024]{2,1,0:T(8,128)S(1)}, f32[4,48,1024]{2,1,0:T(8,128)}, u32[]{:S(2)}, u32[]{:S(2)}) %collective-permute-start) | collective-permute-done | bytes 786464 | tf_op jit(solution)/shard_map/ppermute | solution.py:20
  14.3 0.0 copy-done.2
  14.3 2.3 %fusion = f32[4,48,1024]{2,1,0:T(8,128)S(1)} fusion(f32[4,48,1024]{2,1,0:T(8,128)} %collective-permute-done, f32[4,1024,128]{2,1,0:T(8,128)S(1)} %bitcast.47, f32[128,96]{0,1:T(8,128)S(1)} %copy-done.2, s32[]{:T(128)S(6)} %select_n.27), kind=kOutput, calls=%fused_computation.2 | convolution fusion | flops 151191552 | bytes 3694596 | tf_op jit(solution)/shard_map/jmy,yr->jrm/dot_general | solution.py:21
  16.7 0.0 copy-start.3
  16.7 14.4 %all_to_all.20 = f32[4,48,1024]{2,1,0:T(8,128)S(1)} all-to-all(f32[4,48,1024]{2,1,0:T(8,128)S(1)} %fusion), channel_id=1, replica_groups=mesh['h'=2,'y'=4,'x'=4,'c'=2,'g'=8] {'x'}, dimensions={0} | all-to-all | bytes 1572864 | tf_op jit(solution)/shard_map/all_to_all | solution.py:22
  31.2 0.7 reshape.27
  31.9 10.3 %all-to-all-start.1 = ((f32[16,24,128]{2,1,0:T(8,128)}), f32[16,24,128]{2,1,0:T(8,128)S(1)}, u32[]{:S(2)}, u32[]{:S(2)}) async-start(f32[16,24,128]{2,1,0:T(8,128)} %reshape.27), calls=%async_computation.1 | async-start | bytes 393216 | tf_op jit(solution)/shard_map/all_to_all | solution.py:25
  42.2 0.0 copy-done.3
  42.2 41.6 %all_gather.3 = f32[512,96]{1,0:T(8,128)S(1)} all-gather(f32[64,96]{1,0:T(8,128)S(1)} %copy-done.3), channel_id=1, replica_groups=mesh['h'=2,'y'=4,'x'=4,'c'=2,'g'=8] {'g'}, dimensions={0}, use_global_device_ids=true | all-gather | bytes 221184 | tf_op jit(solution)/shard_map/all_gather | solution.py:14
  83.8 0.0 all-to-all-done.1
  83.8 0.1 reshape.28
  84.0 0.1 copy.5
  84.1 0.3 convolution_bitcast_fusion.3
  84.5 1.0 broadcast_in_dim.3
  85.4 4.9 %all-to-all-start.2 = ((f32[16,96,128]{2,1,0:T(8,128)}), f32[16,96,128]{2,1,0:T(8,128)S(1)}, u32[]{:S(2)}, u32[]{:S(2)}) async-start(f32[16,96,128]{2,1,0:T(8,128)} %broadcast_in_dim.3), calls=%async_computation.2 | async-start | bytes 1572864 | tf_op jit(solution)/shard_map/all_to_all | solution.py:30
  90.4 10.4 %all-to-all-done.2 = f32[16,96,128]{2,1,0:T(8,128)S(1)} async-done(((f32[16,96,128]{2,1,0:T(8,128)}), f32[16,96,128]{2,1,0:T(8,128)S(1)}, u32[]{:S(2)}, u32[]{:S(2)}) %all-to-all-start.2) | async-done | bytes 786464 | tf_op jit(solution)/shard_map/all_to_all | solution.py:30
  100.8 0.0 copy-start.1
  100.8 0.9 copy-done.1
  101.7 1.6 %convolution_bitcast_fusion.2 = f32[2,4,16,2,4,16]{2,5,1,0,3,4:T(8,128)S(1)} fusion(f32[4,4,2,3,16,128]{5,4,3,2,1,0:T(8,128)} %bitcast.49, s32[]{:T(128)S(6)} %select_n.31, s32[]{:T(128)S(6)} %select_n.33, s32[]{:T(128)S(6)} %select_n.29), kind=kOutput, calls=%fused_computation.3 | convolution fusion | flops 37748736 | bytes 458764 | tf_op jit(solution)/shard_map/bjims,khins->bjmhkn/dot_general | solution.py:34
  103.3 0.2 copy.7
  103.6 0.3 reshape.31
  103.8 0.1 reshape.32
  103.9 34.5 %all_to_all.21 = f32[32,4,128]{2,1,0:T(4,128)S(1)} all-to-all(f32[32,4,128]{2,1,0:T(4,128)S(1)} %reshape.32), channel_id=1, replica_groups=mesh['h'=2,'y'=4,'x'=4,'c'=2,'g'=8] {'c','h','g'}, dimensions={0} | all-to-all | bytes 131072 | tf_op jit(solution)/shard_map/all_to_all | solution.py:36
  138.4 0.7 div.23
  (4 shorter events, 0.1 us)
Async XLA Ops:
  0.0 1.6 %copy-start = (f32[64,64,128]{2,1,0:T(8,128)S(1)}, f32[64,64,128]{2,1,0:T(8,128)}, u32[]{:S(2)}) copy-start(f32[64,64,128]{2,1,0:T(8,128)} %param.3) | copy-start | bytes 6291460
  0.0 14.3 %copy-start.2 = (f32[128,96]{0,1:T(8,128)S(1)}, f32[128,96]{0,1:T(8,128)}, u32[]{:S(2)}) copy-start(f32[128,96]{0,1:T(8,128)} %param.4) | copy-start | bytes 147460
  3.5 10.8 %collective-permute-start = (f32[4,48,1024]{2,1,0:T(8,128)S(1)}, f32[4,48,1024]{2,1,0:T(8,128)}, u32[]{:S(2)}, u32[]{:S(2)}) collective-permute-start(f32[4,48,1024]{2,1,0:T(8,128)S(1)} %convolution_bitcast_fusion), channel_id=1, source_target_pairs={{0,8},{8,0},{1,9},{9,1},{2,10},{10,2},{3,11},{11,3},{4,12},{12,4},... | collective-permute-start | bytes 2359304 | tf_op jit(solution)/shard_map/ppermute | solution.py:20
  16.7 25.6 %copy-start.3 = (f32[64,96]{1,0:T(8,128)S(1)}, f32[64,96]{1,0:T(8,128)}, u32[]{:S(2)}) copy-start(f32[64,96]{1,0:T(8,128)} %param.5) | copy-start | bytes 73732
  31.9 52.0 %all-to-all-start.1 = ((f32[16,24,128]{2,1,0:T(8,128)}), f32[16,24,128]{2,1,0:T(8,128)S(1)}, u32[]{:S(2)}, u32[]{:S(2)}) async-start(f32[16,24,128]{2,1,0:T(8,128)} %reshape.27), calls=%async_computation.1 | async-start | bytes 393216 | tf_op jit(solution)/shard_map/all_to_all | solution.py:25
  85.4 15.3 %all-to-all-start.2 = ((f32[16,96,128]{2,1,0:T(8,128)}), f32[16,96,128]{2,1,0:T(8,128)S(1)}, u32[]{:S(2)}, u32[]{:S(2)}) async-start(f32[16,96,128]{2,1,0:T(8,128)} %broadcast_in_dim.3), calls=%async_computation.2 | async-start | bytes 1572864 | tf_op jit(solution)/shard_map/all_to_all | solution.py:30
  100.8 0.9 copy-start.1

commit v2 on v1

v2 whole, which is shorter than its diff:
```python
import jax
import jax.numpy as jnp
from jax import lax
from jax.sharding import Mesh, PartitionSpec as P

R = 96
HIGH = lax.Precision.HIGH
HIGHEST = lax.Precision.HIGHEST


def body(species, factor_y, factor_z):
    y = lax.axis_index("y")
    x = lax.axis_index("x")
    c = lax.axis_index("c")
    four_z = jnp.einsum("ab,zs->azbs", jnp.eye(4, dtype=jnp.float32), factor_z).reshape(256, 384)

    own = species.reshape(4, 16 * 64, 128)
    halves = jnp.stack([
        lax.dynamic_slice(factor_y, (0, (1 - c) * 48), (128, 48)),
        lax.dynamic_slice(factor_y, (0, c * 48), (128, 48)),
    ])
    along_y = jnp.einsum("jmy,qyr->qjrm", own, halves, precision=HIGH)
    along_y = along_y[1] + lax.ppermute(along_y[0], "c", [(0, 1), (1, 0)])
    along_y = lax.all_to_all(along_y, "x", 0, 0, tiled=True).sum(0)

    parts = jnp.einsum("rta,ab->rtb", along_y.reshape(48, 4, 256), four_z, precision=HIGHEST)
    parts = parts.reshape(16, 3, 4, 3, 128).transpose(0, 1, 3, 2, 4).reshape(144, 4, 128)
    parts = lax.all_to_all(parts, ("h", "g"), 0, 0, tiled=True)
    both = parts.reshape(2, 8, 9, 4, 128).sum(1).transpose(1, 0, 2, 3).reshape(9, 8, 128)

    both = jnp.broadcast_to(both, (16, 9, 8, 128)).reshape(144, 8, 128)
    both = lax.all_to_all(both, ("y", "x"), 0, 0, tiled=True)
    both = both.reshape(4, 4, 3, 3, 2, 4, 128)
    rows = lax.dynamic_index_in_dim(both, y, 0, keepdims=False)
    cols = lax.dynamic_slice(both, (2 * (x % 2), 0, 0, 0, x // 2, 0, 0), (2, 4, 3, 3, 1, 4, 128))[:, :, :, :, 0]
    rows = rows.transpose(3, 0, 4, 1, 2, 5).reshape(2, 4, 4, 3, 4, 96)
    cols = cols.transpose(0, 1, 4, 2, 3, 5).reshape(2, 4, 4, 3, 4, 96)
    terms = jnp.einsum("cjtias,hkuibs->cjtahkub", cols, rows, precision=HIGHEST)
    terms = terms.reshape(2, 8, 8, 2, 64).transpose(0, 3, 1, 2, 4).reshape(32, 4, 128)
    terms = lax.all_to_all(terms, ("c", "h", "g"), 0, 0, tiled=True).sum(0)
    return terms.reshape(8, 64).T / (R * R)


def solution(mesh):
    fine = Mesh(mesh.devices.reshape(2, 4, 4, 2, 8), ("h", "y", "x", "c", "g"))
    placed = (P(("h", "y"), "g", ("x", "c")), P(("x", "c"), None), P("g", None))
    return jax.shard_map(
        body, mesh=fine, in_specs=placed, out_specs=P(("h", "y"), ("x", "c", "g")), check_vma=False
    )
```

time: 140 us -> 101 us (0.72)
  blocking collectives: 90.5 us -> 52.4 us
  waiting for transfers between devices: 12.4 us -> 20.9 us
  starting transfers between devices: 24 us -> 17.2 us
  matrix products: 6.23 us -> 2.19 us
    all_gather x1 -> x0, blocking collectives: 41.6 us -> none  [body(): all_z = lax.all_gather(factor_z, 'g', axis=0, tiled=True)]
    all_to_all x2, waiting for transfers between devices: 10.4 us -> 19 us  [the longest x1 9.67 us: body(): along_y = lax.all_to_all(along_y, 'x', 0, 0, tiled=True).sum(0)]
    all_to_all x1, blocking collectives: 14.4 us -> 22.7 us  [body(): parts = lax.all_to_all(parts, ('h', 'g'), 0, 0, tiled=True)]
    all_to_all x2, starting transfers between devices: 15.2 us -> 8.39 us  [the longest x1 4.9 us: body(): both = lax.all_to_all(both, ('y', 'x'), 0, 0, tiled=True)]
    all_to_all x1, blocking collectives: 34.5 us -> 29.6 us  [body(): terms = lax.all_to_all(terms, ('c', 'h', 'g'), 0, 0, tiled=True).sum(0)]
    dot_general x4 -> x3, matrix products: 6.23 us -> 2.19 us  [the longest x1 1.12 us: body(): along_y = jnp.einsum('jmy,qyr->qjrm', own, halves, precision=HIGH)]
    unnamed x8 -> x4, local copies, waits for them, and re-layouts: 2.49 us -> 0.72 us
  transfers between devices with their start and end apart: 3 -> 3, of which waited for: 2 -> 3; matrix products, arithmetic and copies ran while one was open for 0% -> 2% of each run, Pallas kernels for 0% -> 0%
where the time goes in v2:
time: 101 us; the launch traced here: 100 us
  blocking collectives  52.4 us (52%)
  waiting for transfers between devices  20.9 us (21%)
  starting transfers between devices  17.2 us (17%)
  local copies, waits for them, and re-layouts  6.29 us (6%)
  matrix products  2.19 us (2%)
  other arithmetic  1.26 us (1%)
    all_to_all x1, blocking collectives, body(): terms = lax.all_to_all(terms, ('c', 'h', 'g'), 0, 0, tiled=True).sum(0)  29.6 us
    all_to_all x1, blocking collectives, body(): parts = lax.all_to_all(parts, ('h', 'g'), 0, 0, tiled=True)  22.7 us
    all_to_all x1, waiting for transfers between devices, body(): along_y = lax.all_to_all(along_y, 'x', 0, 0, tiled=True).sum(0)  9.67 us
    all_to_all x1, waiting for transfers between devices, body(): both = lax.all_to_all(both, ('y', 'x'), 0, 0, tiled=True)  9.31 us
    ppermute x1, starting transfers between devices, body(): along_y = along_y[1] + lax.ppermute(along_y[0], 'c', [(0, 1), (1, 0)])  8.79 us
    all_to_all x1, starting transfers between devices, body(): both = lax.all_to_all(both, ('y', 'x'), 0, 0, tiled=True)  4.9 us
    all_to_all x1, starting transfers between devices, body(): along_y = lax.all_to_all(along_y, 'x', 0, 0, tiled=True).sum(0)  3.49 us
  transfers between devices with their start and end apart: 3, of which 3 were waited for; matrix products, arithmetic and copies ran while one was open for 2% of the time, Pallas kernels for 0%

profile of v2, /device:TPU:1, one launch (start us, length us, event | category | flops | bytes accessed | tf_op | source)
XLA Modules:
  0.0 100.4 jit_solution(9330377318049794735)
XLA Ops:
  0.0 0.0 copy-start
  0.0 0.9 dynamic-slice_bitcast_fusion.3
  0.9 0.7 copy-done
  1.6 1.1 %convolution_bitcast_fusion = f32[2,4,48,1024]{3,2,1,0:T(8,128)S(1)} fusion(f32[4,1024,128,1]{2,1,0,3:T(8,128)S(1)} %bitcast.66, f32[1,128,48]{1,2,0:T(8,128)S(1)} %get-tuple-element.6, f32[1,128,48]{1,2,0:T(8,128)S(1)} %get-tuple-element.5), kind=kOutput, calls=%fused_computation | convolution fusion | flops 302002176 | bytes 3719168 | tf_op jit(solution)/shard_map/jmy,qyr->qjrm/dot_general | solution.py:22
  2.7 0.1 slice_bitcast_fusion
  2.8 0.0 copy-start.1
  2.8 8.8 %collective-permute-start = (f32[4,48,1024]{2,1,0:T(8,128)S(1)}, f32[4,48,1024]{2,1,0:T(8,128)S(1)}, u32[]{:S(2)}, u32[]{:S(2)}) collective-permute-start(f32[4,48,1024]{2,1,0:T(8,128)S(1)} %slice_bitcast_fusion), channel_id=1, source_target_pairs={{0,8},{8,0},{1,9},{9,1},{2,10},{10,2},{3,11},{11,3},{4,12},{12,4},... | collective-permute-start | bytes 2359304 | tf_op jit(solution)/shard_map/ppermute | solution.py:23
  11.6 1.9 %collective-permute-done = f32[4,48,1024]{2,1,0:T(8,128)S(1)} collective-permute-done((f32[4,48,1024]{2,1,0:T(8,128)S(1)}, f32[4,48,1024]{2,1,0:T(8,128)S(1)}, u32[]{:S(2)}, u32[]{:S(2)}) %collective-permute-start) | collective-permute-done | bytes 786464 | tf_op jit(solution)/shard_map/ppermute | solution.py:23
  13.5 1.0 fusion
  14.5 3.5 %all-to-all-start = ((f32[4,48,1024]{2,1,0:T(8,128)}), f32[4,48,1024]{2,1,0:T(8,128)S(1)}, u32[]{:S(2)}, u32[]{:S(2)}) async-start(f32[4,48,1024]{2,1,0:T(8,128)} %fusion), calls=%async_computation | async-start | bytes 1572864 | tf_op jit(solution)/shard_map/all_to_all | solution.py:24
  18.0 0.0 copy-done.1
  18.0 0.1 multiply_bitcast_fusion
  18.2 1.0 %reshape.42 = f32[256,384]{1,0:T(8,128)} reshape(f32[4,64,4,96]{3,2,1,0:T(4,128)S(1)} %multiply_bitcast_fusion) | data formatting | bytes 786432 | tf_op jit(solution)/shard_map/reshape | solution.py:15
  19.2 1.2 %copy.21 = f32[384,256]{1,0:T(8,128)S(1)} copy(f32[384,256]{0,1:T(8,128)} %bitcast.68) | data formatting | bytes 786432 | tf_op jit(solution)/shard_map/rta,ab->rtb/dot_general | solution.py:26
  20.3 9.7 %all-to-all-done = f32[4,48,1024]{2,1,0:T(8,128)S(1)} async-done(((f32[4,48,1024]{2,1,0:T(8,128)}), f32[4,48,1024]{2,1,0:T(8,128)S(1)}, u32[]{:S(2)}, u32[]{:S(2)}) %all-to-all-start) | async-done | bytes 786464 | tf_op jit(solution)/shard_map/all_to_all | solution.py:24
  30.0 0.1 dot_general.31
  30.1 0.5 convolution_bitcast_fusion.1
  30.7 0.1 copy.23
  30.8 22.7 %all_to_all.20 = f32[144,4,128]{2,1,0:T(4,128)S(1)} all-to-all(f32[144,4,128]{2,1,0:T(4,128)S(1)} %bitcast.71), channel_id=1, replica_groups=mesh['h'=2,'y'=4,'x'=4,'c'=2,'g'=8] {'h','g'}, dimensions={0} | all-to-all | bytes 589824 | tf_op jit(solution)/shard_map/all_to_all | solution.py:28
  53.6 0.1 reduce_sum.28
  53.6 0.8 broadcast_in_dim.3
  54.5 4.9 %all-to-all-start.2 = ((f32[144,8,128]{2,1,0:T(8,128)}), f32[144,8,128]{2,1,0:T(8,128)S(1)}, u32[]{:S(2)}, u32[]{:S(2)}) async-start(f32[144,8,128]{2,1,0:T(8,128)} %bitcast.20), calls=%async_computation.2 | async-start | bytes 1179648 | tf_op jit(solution)/shard_map/all_to_all | solution.py:32
  59.4 9.3 %all-to-all-done.2 = f32[144,8,128]{2,1,0:T(8,128)S(1)} async-done(((f32[144,8,128]{2,1,0:T(8,128)}), f32[144,8,128]{2,1,0:T(8,128)S(1)}, u32[]{:S(2)}, u32[]{:S(2)}) %all-to-all-start.2) | async-done | bytes 589856 | tf_op jit(solution)/shard_map/all_to_all | solution.py:32
  68.8 0.1 copy.25
  68.8 0.2 reshape.48
  69.1 0.1 copy.27
  69.1 0.2 reshape.49
  69.4 0.5 convolution_bitcast_fusion.2
  69.9 0.1 reshape.50
  70.0 29.6 %all_to_all.21 = f32[32,4,128]{2,1,0:T(4,128)S(1)} all-to-all(f32[32,4,128]{2,1,0:T(4,128)S(1)} %reshape.50), channel_id=1, replica_groups=mesh['h'=2,'y'=4,'x'=4,'c'=2,'g'=8] {'c','h','g'}, dimensions={0} | all-to-all | bytes 131072 | tf_op jit(solution)/shard_map/all_to_all | solution.py:40
  99.7 0.7 div.23
  (10 shorter events, 0.2 us)
Async XLA Ops:
  0.0 1.6 %copy-start = (f32[64,64,128]{2,1,0:T(8,128)S(1)}, f32[64,64,128]{2,1,0:T(8,128)}, u32[]{:S(2)}) copy-start(f32[64,64,128]{2,1,0:T(8,128)} %param.3) | copy-start | bytes 6291460
  2.8 15.2 %copy-start.1 = (f32[64,96]{1,0:T(8,128)S(1)}, f32[64,96]{1,0:T(8,128)}, u32[]{:S(2)}) copy-start(f32[64,96]{1,0:T(8,128)} %param.5) | copy-start | bytes 73732
  2.8 10.7 %collective-permute-start = (f32[4,48,1024]{2,1,0:T(8,128)S(1)}, f32[4,48,1024]{2,1,0:T(8,128)S(1)}, u32[]{:S(2)}, u32[]{:S(2)}) collective-permute-start(f32[4,48,1024]{2,1,0:T(8,128)S(1)} %slice_bitcast_fusion), channel_id=1, source_target_pairs={{0,8},{8,0},{1,9},{9,1},{2,10},{10,2},{3,11},{11,3},{4,12},{12,4},... | collective-permute-start | bytes 2359304 | tf_op jit(solution)/shard_map/ppermute | solution.py:23
  14.5 15.5 %all-to-all-start = ((f32[4,48,1024]{2,1,0:T(8,128)}), f32[4,48,1024]{2,1,0:T(8,128)S(1)}, u32[]{:S(2)}, u32[]{:S(2)}) async-start(f32[4,48,1024]{2,1,0:T(8,128)} %fusion), calls=%async_computation | async-start | bytes 1572864 | tf_op jit(solution)/shard_map/all_to_all | solution.py:24
  54.5 14.2 %all-to-all-start.2 = ((f32[144,8,128]{2,1,0:T(8,128)}), f32[144,8,128]{2,1,0:T(8,128)S(1)}, u32[]{:S(2)}, u32[]{:S(2)}) async-start(f32[144,8,128]{2,1,0:T(8,128)} %bitcast.20), calls=%async_computation.2 | async-start | bytes 1179648 | tf_op jit(solution)/shard_map/all_to_all | solution.py:32

commit v3 on v0

v3 whole, which is shorter than its diff:
```python
import jax
import jax.numpy as jnp
from jax import lax
from jax.experimental import pallas as pl
from jax.experimental.pallas import tpu as pltpu
from jax.sharding import Mesh, PartitionSpec as P

R = 96
HIGHEST = lax.Precision.HIGHEST
F32 = jnp.float32
BF16 = jnp.bfloat16
PARAMS = pltpu.CompilerParams(vmem_limit_bytes=32 * 1024 * 1024)


def split(value):
    top = value.astype(BF16)
    return top, (value - top.astype(F32)).astype(BF16)


def dot_nt(left, right):
    return lax.dot_general(left, right, (((1,), (1,)), ((), ())), preferred_element_type=F32)


def y_kernel(species_hbm, factor_hbm, others_ref, mine_ref, field_ref, factor_ref, left_ref, sems):
    c = lax.axis_index("c")
    copies = [pltpu.make_async_copy(factor_hbm, factor_ref, sems.at[4])]
    for j in range(4):
        rows = pl.ds(16 * j, 16)
        copies.append(pltpu.make_async_copy(species_hbm.at[rows], field_ref.at[rows], sems.at[j]))
    for copy in copies:
        copy.start()
    copies[0].wait()
    top, low = split(factor_ref[...])
    left_ref[0:R, 0:128] = top
    left_ref[0:R, 128:256] = top
    left_ref[R:192, 0:128] = low
    left_ref[R:192, 128:256] = jnp.zeros_like(low)
    for j in range(4):
        copies[1 + j].wait()
        top, low = split(field_ref[16 * j : 16 * j + 16].reshape(1024, 128))
        both = dot_nt(left_ref[...], jnp.concatenate([top, low], axis=1))
        both = both[0:R] + both[R:192]

        @pl.when(c == 0)
        def _():
            mine_ref[j] = both[0:48]
            others_ref[j] = both[48:96]

        @pl.when(c == 1)
        def _():
            others_ref[j] = both[0:48]
            mine_ref[j] = both[48:96]


def y_product(species, factor_y):
    half = jax.ShapeDtypeStruct((4, 48, 1024), F32)
    hbm = pl.BlockSpec(memory_space=pltpu.HBM)
    return pl.pallas_call(
        y_kernel,
        in_specs=[hbm, hbm],
        out_shape=[half, half],
        scratch_shapes=[
            pltpu.VMEM((64, 64, 128), F32),
            pltpu.VMEM((R, 128), F32),
            pltpu.VMEM((192, 256), BF16),
            pltpu.SemaphoreType.DMA((5,)),
        ],
        compiler_params=PARAMS,
    )(pltpu.with_memory_space_constraint(species, pltpu.HBM), pltpu.with_memory_space_constraint(factor_y.T, pltpu.HBM))


def add_kernel(a_ref, b_ref, out_ref):
    out_ref[...] = a_ref[...] + b_ref[...]


def add(a, b):
    return pl.pallas_call(
        add_kernel, out_shape=pltpu.VMEM(a.shape, F32), compiler_params=PARAMS
    )(a, b)


def z_kernel(parts_ref, factor_ref, out_ref):
    rows = []
    for t in range(4):
        lanes = slice(256 * t, 256 * t + 256)
        rows.append((parts_ref[0, :, lanes] + parts_ref[1, :, lanes]) + (parts_ref[2, :, lanes] + parts_ref[3, :, lanes]))
    top, low = split(jnp.concatenate(rows, axis=0))
    factor, rest = split(factor_ref[...])
    both = jnp.dot(jnp.concatenate([top, low], axis=0), factor, preferred_element_type=F32)
    both = both[0:192] + both[192:384] + jnp.dot(top, rest, preferred_element_type=F32)
    for t in range(4):
        for k in range(3):
            out_ref[pl.ds(4 * k + t, 48, stride=12), :] = both[48 * t : 48 * t + 48, 128 * k : 128 * k + 128]


def z_product(parts, factor):
    return pl.pallas_call(
        z_kernel, out_shape=jax.ShapeDtypeStruct((576, 128), F32), compiler_params=PARAMS
    )(parts, factor)


def copies_kernel(parts_ref, out_ref, both_ref):
    for h in range(2):
        both_ref[:, 4 * h : 4 * h + 4] = parts_ref[h].sum(0)
    for n in range(16):
        out_ref[n] = both_ref[...]


def copies(parts):
    return pl.pallas_call(
        copies_kernel,
        out_shape=jax.ShapeDtypeStruct((16, 9, 8, 128), F32),
        scratch_shapes=[pltpu.VMEM((9, 8, 128), F32)],
        compiler_params=PARAMS,
    )(parts)


def gram_kernel(both_ref, out_ref, terms_ref):
    x, y = lax.axis_index("x"), lax.axis_index("y")

    def rows_of(start, count, i):
        tiles = [both_ref[pl.ds(start, count), 3 * i + k].reshape(8 * count, 128) for k in range(3)]
        wide = jnp.concatenate(tiles, axis=1)
        return split(jnp.concatenate([wide[:, R * q : R * q + R] for q in range(4)], axis=0))

    total = jnp.zeros((256, 128), F32)
    for i in range(3):
        top, low = rows_of(8 * (x % 2), 8, i)
        right, rest = rows_of(4 * y, 4, i)
        total += dot_nt(top, right) + (dot_nt(low, right) + dot_nt(top, rest))
    terms_ref[...] = total
    first = (lax.broadcasted_iota(jnp.int32, (4, 128), 1) & 4) == 0
    for c in range(2):
        for k in range(4):
            for t in range(0, 4, 2):
                start = 32 * c + 8 * k + t + 4 * (x // 2)
                even = terms_ref[pl.ds(start, 4, stride=64), :]
                odd = terms_ref[pl.ds(start + 1, 4, stride=64), :]
                out_ref[c, 0, 2 * k + t // 2] = jnp.where(first, even, pltpu.roll(odd, 4, 1))
                out_ref[c, 1, 2 * k + t // 2] = jnp.where(first, pltpu.roll(even, 124, 1), odd)


def gram_terms(both):
    return pl.pallas_call(
        gram_kernel,
        out_shape=jax.ShapeDtypeStruct((2, 2, 8, 4, 128), F32),
        scratch_shapes=[pltpu.VMEM((256, 128), F32)],
        compiler_params=PARAMS,
    )(both)


def last_kernel(terms_ref, out_ref):
    total = terms_ref[...].sum(0)
    row = lax.broadcasted_iota(jnp.int32, (64, 128), 0)
    lane = lax.broadcasted_iota(jnp.int32, (64, 128), 1)
    source = (row & 3) * 32 + (row >> 4) * 8 + ((row >> 2) & 3)
    for half in range(2):
        pick = jnp.where(lane == source + 4 * half, 1.0, 0.0).astype(F32)
        moved = lax.dot_general(total, pick, (((1,), (1,)), ((), ())), precision=HIGHEST, preferred_element_type=F32)
        out_ref[4 * half : 4 * half + 4] = moved / (R * R)


def last(terms):
    return pl.pallas_call(
        last_kernel, out_shape=jax.ShapeDtypeStruct((8, 64), F32), compiler_params=PARAMS
    )(terms).T


def body(species, factor_y, factor_z):
    four_z = jnp.einsum("ab,zs->azbs", jnp.eye(4, dtype=F32), factor_z).reshape(256, 384)
    others, mine = y_product(species, factor_y)
    along_y = add(mine, lax.ppermute(others, "c", [(0, 1), (1, 0)]))
    parts = z_product(lax.all_to_all(along_y, "x", 0, 0, tiled=True), four_z)
    parts = lax.all_to_all(parts.reshape(144, 4, 128), ("h", "g"), 0, 0, tiled=True)
    both = copies(parts.reshape(2, 8, 9, 4, 128)).reshape(144, 8, 128)
    both = lax.all_to_all(both, ("y", "x"), 0, 0, tiled=True)
    terms = gram_terms(both.reshape(16, 9, 8, 128)).reshape(32, 4, 128)
    return last(lax.all_to_all(terms, ("c", "h", "g"), 0, 0, tiled=True))


def solution(mesh):
    fine = Mesh(mesh.devices.reshape(2, 4, 4, 2, 8), ("h", "y", "x", "c", "g"))
    placed = (P(("h", "y"), "g", ("x", "c")), P(("x", "c"), None), P("g", None))
    return jax.shard_map(
        body, mesh=fine, in_specs=placed, out_specs=P(("h", "y"), ("x", "c", "g")), check_vma=False
    )
```

time: 987 us -> 98.3 us (0.10); the launches traced: 974 us -> 98 us
  waiting for transfers between devices: 880 us -> 13.5 us
  between operations: 13.8 us -> 0.08 us
  starting transfers between devices: 0.09 us -> 12.2 us
    unnamed x4 -> x0, waiting for transfers between devices: 771 us -> none
    reduce_scatter x2 -> x0, waiting for transfers between devices: 108 us -> none  [the longest x1 61.7 us: body(): block = lax.psum_scatter(both, 'gz', scatter_dimension=1, tiled=True)]
    all_to_all x0 -> x3, blocking collectives: none -> 66.4 us  [the longest x1 29.6 us: body(): return last(lax.all_to_all(terms, ('c', 'h', 'g'), 0, 0, tiled=True))]
    all_gather x1 -> x0, blocking collectives: 60.7 us -> none  [body(): lax.all_gather(own_rows, 'gx', axis=0, tiled=True)]
    all_to_all x0 -> x1, waiting for transfers between devices: none -> 11.6 us  [body(): parts = z_product(lax.all_to_all(along_y, 'x', 0, 0, tiled=True), four_z)]
  transfers between devices with their start and end apart: 3 -> 2, of which waited for: 3 -> 2; matrix products, arithmetic and copies ran while one was open for 0% -> 0% of each run, Pallas kernels for 0% -> 0%
where the time goes in v3:
time: 98.3 us; the launch traced here: 98 us
  blocking collectives  66.4 us (68%)
  waiting for transfers between devices  13.5 us (14%)
  starting transfers between devices  12.2 us (12%)
  Pallas kernels  5.35 us (5%)
    all_to_all x1, blocking collectives, body(): return last(lax.all_to_all(terms, ('c', 'h', 'g'), 0, 0, tiled=True))  29.6 us
    all_to_all x1, blocking collectives, body(): lax.all_to_all(parts.reshape(144, 4, 128), ('h', 'g'), 0, 0, tiled=True)  22.7 us
    all_to_all x1, blocking collectives, body(): both = lax.all_to_all(both, ('y', 'x'), 0, 0, tiled=True)  14.1 us
    all_to_all x1, waiting for transfers between devices, body(): parts = z_product(lax.all_to_all(along_y, 'x', 0, 0, tiled=True), four_z)  11.6 us
    ppermute x1, starting transfers between devices, body(): along_y = add(mine, lax.ppermute(others, 'c', [(0, 1), (1, 0)]))  8.72 us
    all_to_all x1, starting transfers between devices, body(): parts = z_product(lax.all_to_all(along_y, 'x', 0, 0, tiled=True), four_z)  3.49 us
    pallas_call x1, Pallas kernels, y_product(): pl.pallas_call(y_kernel, in_specs=[hbm, hbm], out_shape=[half, half], scr...  2.56 us
  transfers between devices with their start and end apart: 2, of which 2 were waited for; matrix products, arithmetic and copies ran while one was open for 0% of the time, Pallas kernels for 0%

profile of v3, /device:TPU:1, one launch (start us, length us, event | category | flops | bytes accessed | tf_op | source)
XLA Modules:
  0.0 98.0 jit_solution(8717809893621950117)
XLA Ops:
  0.0 2.6 %shard_map.37 = (f32[4,48,1024]{2,1,0:T(8,128)S(1)}, f32[4,48,1024]{2,1,0:T(8,128)S(1)}) custom-call(f32[64,64,128]{2,1,0:T(8,128)} %species_hbm.1, f32[96,128]{1,0:T(8,128)} %bitcast.14), custom_call_target="tpu_custom_call" | custom-call | tf_op jit(solution)/shard_map/pallas_call | solution.py:58
  2.6 0.0 copy-start
  2.6 8.7 %collective-permute-start = (f32[4,48,1024]{2,1,0:T(8,128)S(1)}, f32[4,48,1024]{2,1,0:T(8,128)S(1)}, u32[]{:S(2)}, u32[]{:S(2)}) collective-permute-start(f32[4,48,1024]{2,1,0:T(8,128)S(1)} %get-tuple-element.8), channel_id=1, source_target_pairs={{0,8},{8,0},{1,9},{9,1},{2,10},{10,2},{3,11},{11,3},{4,12},{12,4},... | collective-permute-start | bytes 2359304 | tf_op jit(solution)/shard_map/ppermute | solution.py:172
  11.3 1.9 %collective-permute-done.b_ref = f32[4,48,1024]{2,1,0:T(8,128)S(1)} collective-permute-done((f32[4,48,1024]{2,1,0:T(8,128)S(1)}, f32[4,48,1024]{2,1,0:T(8,128)S(1)}, u32[]{:S(2)}, u32[]{:S(2)}) %collective-permute-start) | collective-permute-done | bytes 786464 | tf_op jit(solution)/shard_map/ppermute | solution.py:172
  13.2 1.0 shard_map.38
  14.2 3.5 %all-to-all-start = ((f32[4,48,1024]{2,1,0:T(8,128)}), f32[4,48,1024]{2,1,0:T(8,128)S(1)}, u32[]{:S(2)}, u32[]{:S(2)}) async-start(f32[4,48,1024]{2,1,0:T(8,128)} %shard_map.38), calls=%async_computation | async-start | bytes 1572864 | tf_op jit(solution)/shard_map/all_to_all | solution.py:173
  17.7 0.0 copy-done
  17.7 0.1 multiply_bitcast_fusion
  17.8 0.3 reshape.18.factor_ref
  18.1 11.6 %all-to-all-done.parts_ref = f32[4,48,1024]{2,1,0:T(8,128)S(1)} async-done(((f32[4,48,1024]{2,1,0:T(8,128)}), f32[4,48,1024]{2,1,0:T(8,128)S(1)}, u32[]{:S(2)}, u32[]{:S(2)}) %all-to-all-start) | async-done | bytes 786464 | tf_op jit(solution)/shard_map/all_to_all | solution.py:173
  29.7 0.3 shard_map.39
  30.0 22.7 %all_to_all.20 = f32[144,4,128]{2,1,0:T(4,128)S(1)} all-to-all(f32[144,4,128]{2,1,0:T(4,128)S(1)} %bitcast.12), channel_id=1, replica_groups=mesh['h'=2,'y'=4,'x'=4,'c'=2,'g'=8] {'h','g'}, dimensions={0} | all-to-all | bytes 589824 | tf_op jit(solution)/shard_map/all_to_all | solution.py:174
  52.8 0.1 shard_map.40
  52.8 14.1 %all_to_all.21 = f32[144,8,128]{2,1,0:T(8,128)S(1)} all-to-all(f32[144,8,128]{2,1,0:T(8,128)S(1)} %bitcast.9), channel_id=1, replica_groups=mesh['h'=2,'y'=4,'x'=4,'c'=2,'g'=8] {'y','x'}, dimensions={0} | all-to-all | bytes 1179648 | tf_op jit(solution)/shard_map/all_to_all | solution.py:176
  66.9 0.5 shard_map.41
  67.5 29.6 %all_to_all.22.terms_ref = f32[32,4,128]{2,1,0:T(4,128)S(1)} all-to-all(f32[32,4,128]{2,1,0:T(4,128)S(1)} %bitcast.13), channel_id=1, replica_groups=mesh['h'=2,'y'=4,'x'=4,'c'=2,'g'=8] {'c','h','g'}, dimensions={0} | all-to-all | bytes 131072 | tf_op jit(solution)/shard_map/all_to_all | solution.py:178
  97.1 0.8 shard_map.42
  (1 shorter events, 0.0 us)
Async XLA Ops:
  2.6 15.1 %copy-start = (f32[64,96]{1,0:T(8,128)S(1)}, f32[64,96]{1,0:T(8,128)}, u32[]{:S(2)}) copy-start(f32[64,96]{1,0:T(8,128)} %param.5) | copy-start | bytes 73732
  2.6 10.6 %collective-permute-start = (f32[4,48,1024]{2,1,0:T(8,128)S(1)}, f32[4,48,1024]{2,1,0:T(8,128)S(1)}, u32[]{:S(2)}, u32[]{:S(2)}) collective-permute-start(f32[4,48,1024]{2,1,0:T(8,128)S(1)} %get-tuple-element.8), channel_id=1, source_target_pairs={{0,8},{8,0},{1,9},{9,1},{2,10},{10,2},{3,11},{11,3},{4,12},{12,4},... | collective-permute-start | bytes 2359304 | tf_op jit(solution)/shard_map/ppermute | solution.py:172
  14.2 15.5 %all-to-all-start = ((f32[4,48,1024]{2,1,0:T(8,128)}), f32[4,48,1024]{2,1,0:T(8,128)S(1)}, u32[]{:S(2)}, u32[]{:S(2)}) async-start(f32[4,48,1024]{2,1,0:T(8,128)} %shard_map.38), calls=%async_computation | async-start | bytes 1572864 | tf_op jit(solution)/shard_map/all_to_all | solution.py:173

commit v4 on v3

--- a/solution.py
+++ b/solution.py
@@ -21,7 +21,18 @@
     return lax.dot_general(left, right, (((1,), (1,)), ((), ())), preferred_element_type=F32)
 
 
-def y_kernel(species_hbm, factor_hbm, others_ref, mine_ref, field_ref, factor_ref, left_ref, sems):
+def halves(rows):
+    top, low = split(rows)
+    upper = jnp.concatenate([top, top], axis=1)
+    return jnp.concatenate([upper, jnp.concatenate([low, jnp.zeros_like(low)], axis=1)], axis=0)
+
+
+def product(left, right):
+    both = dot_nt(left, right)
+    return both[0:48] + both[48:96]
+
+
+def others_kernel(species_hbm, factor_hbm, others_ref, right_ref, left_ref, field_ref, factor_ref, sems):
     c = lax.axis_index("c")
     copies = [pltpu.make_async_copy(factor_hbm, factor_ref, sems.at[4])]
     for j in range(4):
@@ -30,73 +41,93 @@
     for copy in copies:
         copy.start()
     copies[0].wait()
-    top, low = split(factor_ref[...])
-    left_ref[0:R, 0:128] = top
-    left_ref[0:R, 128:256] = top
-    left_ref[R:192, 0:128] = low
-    left_ref[R:192, 128:256] = jnp.zeros_like(low)
+    left_ref[...] = halves(factor_ref[pl.ds(pl.multiple_of(48 * c, 48), 48)])
+    left = halves(factor_ref[pl.ds(pl.multiple_of(48 * (1 - c), 48), 48)])
     for j in range(4):
         copies[1 + j].wait()
         top, low = split(field_ref[16 * j : 16 * j + 16].reshape(1024, 128))
-        both = dot_nt(left_ref[...], jnp.concatenate([top, low], axis=1))
-        both = both[0:R] + both[R:192]
-
-        @pl.when(c == 0)
-        def _():
-            mine_ref[j] = both[0:48]
-            others_ref[j] = both[48:96]
-
-        @pl.when(c == 1)
-        def _():
-            others_ref[j] = both[0:48]
-            mine_ref[j] = both[48:96]
-
-
-def y_product(species, factor_y):
-    half = jax.ShapeDtypeStruct((4, 48, 1024), F32)
+        right = jnp.concatenate([top, low], axis=1)
+        right_ref[j] = right
+        others_ref[j] = product(left, right)
+
+
+def others_product(species, factor_y):
     hbm = pl.BlockSpec(memory_space=pltpu.HBM)
     return pl.pallas_call(
-        y_kernel,
+        others_kernel,
         in_specs=[hbm, hbm],
-        out_shape=[half, half],
+        out_shape=[
+            jax.ShapeDtypeStruct((4, 48, 1024), F32),
+            pltpu.VMEM((4, 1024, 256), BF16),
+            pltpu.VMEM((96, 256), BF16),
+        ],
         scratch_shapes=[
             pltpu.VMEM((64, 64, 128), F32),
             pltpu.VMEM((R, 128), F32),
-            pltpu.VMEM((192, 256), BF16),
             pltpu.SemaphoreType.DMA((5,)),
         ],
         compiler_params=PARAMS,
     )(pltpu.with_memory_space_constraint(species, pltpu.HBM), pltpu.with_memory_space_constraint(factor_y.T, pltpu.HBM))
 
 
-def add_kernel(a_ref, b_ref, out_ref):
-    out_ref[...] = a_ref[...] + b_ref[...]
-
-
-def add(a, b):
-    return pl.pallas_call(
-        add_kernel, out_shape=pltpu.VMEM(a.shape, F32), compiler_params=PARAMS
-    )(a, b)
-
-
-def z_kernel(parts_ref, factor_ref, out_ref):
+def early_kernel(left_ref, right_ref, factor_ref, out_ref, top_ref, low_ref, four_ref):
+    four_ref[...] = jnp.zeros_like(four_ref)
+    for q in range(4):
+        four_ref[64 * q : 64 * q + 64, R * q : R * q + R] = factor_ref[...]
+    top_ref[...], low_ref[...] = split(four_ref[...])
+
+    @pl.when(lax.axis_index("c") == 1)
+    def _():
+        for j in range(4):
+            out_ref[j] = product(left_ref[...], right_ref[j])
+
+
+def early_product(left, right, factor_z):
+    four = pltpu.VMEM((256, 384), BF16)
+    return pl.pallas_call(
+        early_kernel,
+        out_shape=[pltpu.VMEM((4, 48, 1024), F32), four, four],
+        scratch_shapes=[pltpu.VMEM((256, 384), F32)],
+        compiler_params=PARAMS,
+    )(left, right, factor_z)
+
+
+def add_kernel(left_ref, right_ref, mine_ref, received_ref, out_ref):
+    c = lax.axis_index("c")
+
+    @pl.when(c == 0)
+    def _():
+        for j in range(4):
+            out_ref[j] = product(left_ref[...], right_ref[j]) + received_ref[j]
+
+    @pl.when(c == 1)
+    def _():
+        out_ref[...] = mine_ref[...] + received_ref[...]
+
+
+def add(left, right, mine, received):
+    return pl.pallas_call(
+        add_kernel, out_shape=pltpu.VMEM(mine.shape, F32), compiler_params=PARAMS
+    )(left, right, mine, received)
+
+
+def z_kernel(parts_ref, factor_ref, rest_ref, out_ref):
     rows = []
     for t in range(4):
         lanes = slice(256 * t, 256 * t + 256)
         rows.append((parts_ref[0, :, lanes] + parts_ref[1, :, lanes]) + (parts_ref[2, :, lanes] + parts_ref[3, :, lanes]))
     top, low = split(jnp.concatenate(rows, axis=0))
-    factor, rest = split(factor_ref[...])
-    both = jnp.dot(jnp.concatenate([top, low], axis=0), factor, preferred_element_type=F32)
-    both = both[0:192] + both[192:384] + jnp.dot(top, rest, preferred_element_type=F32)
+    both = jnp.dot(jnp.concatenate([top, low], axis=0), factor_ref[...], preferred_element_type=F32)
+    both = both[0:192] + both[192:384] + jnp.dot(top, rest_ref[...], preferred_element_type=F32)
     for t in range(4):
         for k in range(3):
             out_ref[pl.ds(4 * k + t, 48, stride=12), :] = both[48 * t : 48 * t + 48, 128 * k : 128 * k + 128]
 
 
-def z_product(parts, factor):
+def z_product(parts, factor, rest):
     return pl.pallas_call(
         z_kernel, out_shape=jax.ShapeDtypeStruct((576, 128), F32), compiler_params=PARAMS
-    )(parts, factor)
+    )(parts, factor, rest)
 
 
 def copies_kernel(parts_ref, out_ref, both_ref):
@@ -167,10 +198,10 @@
 
 
 def body(species, factor_y, factor_z):
-    four_z = jnp.einsum("ab,zs->azbs", jnp.eye(4, dtype=F32), factor_z).reshape(256, 384)
-    others, mine = y_product(species, factor_y)
-    along_y = add(mine, lax.ppermute(others, "c", [(0, 1), (1, 0)]))
-    parts = z_product(lax.all_to_all(along_y, "x", 0, 0, tiled=True), four_z)
+    others, right, left = others_product(species, factor_y)
+    mine, factor, rest = early_product(left, right, factor_z)
+    along_y = add(left, right, mine, lax.ppermute(others, "c", [(0, 1), (1, 0)]))
+    parts = z_product(lax.all_to_all(along_y, "x", 0, 0, tiled=True), factor, rest)
     parts = lax.all_to_all(parts.reshape(144, 4, 128), ("h", "g"), 0, 0, tiled=True)
     both = copies(parts.reshape(2, 8, 9, 4, 128)).reshape(144, 8, 128)
     both = lax.all_to_all(both, ("y", "x"), 0, 0, tiled=True)

time: 98.3 us -> 95.5 us (0.972)
  blocking collectives: 66.4 us -> 80.3 us
  waiting for transfers between devices: 13.5 us -> 1.01 us
  starting transfers between devices: 12.2 us -> 8.78 us
    all_to_all x0 -> x1, blocking collectives: none -> 13.7 us  [body(): lax.all_to_all(along_y, 'x', 0, 0, tiled=True)]
    all_to_all x1 -> x0, waiting for transfers between devices: 11.6 us -> none  [body(): parts = z_product(lax.all_to_all(along_y, 'x', 0, 0, tiled=True), four_z)]
    all_to_all x1 -> x0, starting transfers between devices: 3.49 us -> none  [body(): parts = z_product(lax.all_to_all(along_y, 'x', 0, 0, tiled=True), four_z)]
    pallas_call x2 -> x3, Pallas kernels: 3.52 us -> 3.26 us  [the longest x1 2.32 us: others_product(): pl.pallas_call(others_kernel, in_specs=[hbm, hbm], out_shape=[jax.ShapeDt...]
  transfers between devices with their start and end apart: 2 -> 1, of which waited for: 2 -> 1; matrix products, arithmetic and copies ran while one was open for 0% -> 0% of each run, Pallas kernels for 0% -> 1%
where the time goes in v4:
time: 95.5 us; the launch traced here: 95.2 us
  blocking collectives  80.3 us (84%)
  starting transfers between devices  8.78 us (9%)
  Pallas kernels  5.07 us (5%)
  waiting for transfers between devices  1.01 us (1%)
    all_to_all x1, blocking collectives, body(): return last(lax.all_to_all(terms, ('c', 'h', 'g'), 0, 0, tiled=True))  29.3 us
    all_to_all x1, blocking collectives, body(): lax.all_to_all(parts.reshape(144, 4, 128), ('h', 'g'), 0, 0, tiled=True)  23.3 us
    all_to_all x1, blocking collectives, body(): both = lax.all_to_all(both, ('y', 'x'), 0, 0, tiled=True)  14.1 us
    all_to_all x1, blocking collectives, body(): lax.all_to_all(along_y, 'x', 0, 0, tiled=True)  13.7 us
    ppermute x1, starting transfers between devices, body(): lax.ppermute(others, 'c', [(0, 1), (1, 0)])  8.78 us
    pallas_call x1, Pallas kernels, others_product(): pl.pallas_call(others_kernel, in_specs=[hbm, hbm], out_shape=[jax.ShapeDt...  2.32 us
  transfers between devices with their start and end apart: 1, of which 1 were waited for; matrix products, arithmetic and copies ran while one was open for 0% of the time, Pallas kernels for 1%

profile of v4, /device:TPU:1, one launch (start us, length us, event | category | flops | bytes accessed | tf_op | source)
XLA Modules:
  0.0 95.2 jit_solution(3647158090372912419)
XLA Ops:
  0.0 0.0 copy-start
  0.0 2.3 %shard_map.37 = (f32[4,48,1024]{2,1,0:T(8,128)S(1)}, bf16[4,1024,256]{2,1,0:T(8,128)(2,1)S(1)}, bf16[96,256]{1,0:T(8,128)(2,1)S(1)}) custom-call(f32[64,64,128]{2,1,0:T(8,128)} %species_hbm.1, f32[96,128]{1,0:T(8,128)} %bitcast.12), custom_call_target="tpu_custom_call" | custom-call | tf_op jit(solution)/shard_map/pallas_call | solution.py:56
  2.3 8.8 %collective-permute-start = (f32[4,48,1024]{2,1,0:T(8,128)S(1)}, f32[4,48,1024]{2,1,0:T(8,128)S(1)}, u32[]{:S(2)}, u32[]{:S(2)}) collective-permute-start(f32[4,48,1024]{2,1,0:T(8,128)S(1)} %get-tuple-element.14), channel_id=1, source_target_pairs={{0,8},{8,0},{1,9},{9,1},{2,10},{10,2},{3,11},{11,3},{4,12},{12,4},... | collective-permute-start | bytes 2359304 | tf_op jit(solution)/shard_map/ppermute | solution.py:203
  11.1 0.0 copy-done
  11.1 0.9 shard_map.38
  12.0 1.0 %collective-permute-done.received_ref = f32[4,48,1024]{2,1,0:T(8,128)S(1)} collective-permute-done((f32[4,48,1024]{2,1,0:T(8,128)S(1)}, f32[4,48,1024]{2,1,0:T(8,128)S(1)}, u32[]{:S(2)}, u32[]{:S(2)}) %collective-permute-start) | collective-permute-done | bytes 786464 | tf_op jit(solution)/shard_map/ppermute | solution.py:203
  13.0 0.1 shard_map.39
  13.1 13.7 %all_to_all.20.parts_ref = f32[4,48,1024]{2,1,0:T(8,128)S(1)} all-to-all(f32[4,48,1024]{2,1,0:T(8,128)S(1)} %shard_map.39), channel_id=1, replica_groups=mesh['h'=2,'y'=4,'x'=4,'c'=2,'g'=8] {'x'}, dimensions={0} | all-to-all | bytes 1572864 | tf_op jit(solution)/shard_map/all_to_all | solution.py:204
  26.8 0.3 shard_map.40
  27.1 23.3 %all_to_all.21 = f32[144,4,128]{2,1,0:T(4,128)S(1)} all-to-all(f32[144,4,128]{2,1,0:T(4,128)S(1)} %bitcast.10), channel_id=1, replica_groups=mesh['h'=2,'y'=4,'x'=4,'c'=2,'g'=8] {'h','g'}, dimensions={0} | all-to-all | bytes 589824 | tf_op jit(solution)/shard_map/all_to_all | solution.py:205
  50.4 0.1 shard_map.41
  50.4 14.1 %all_to_all.22 = f32[144,8,128]{2,1,0:T(8,128)S(1)} all-to-all(f32[144,8,128]{2,1,0:T(8,128)S(1)} %bitcast.7), channel_id=1, replica_groups=mesh['h'=2,'y'=4,'x'=4,'c'=2,'g'=8] {'y','x'}, dimensions={0} | all-to-all | bytes 1179648 | tf_op jit(solution)/shard_map/all_to_all | solution.py:207
  64.5 0.5 shard_map.42
  65.1 29.3 %all_to_all.23.terms_ref = f32[32,4,128]{2,1,0:T(4,128)S(1)} all-to-all(f32[32,4,128]{2,1,0:T(4,128)S(1)} %bitcast.11), channel_id=1, replica_groups=mesh['h'=2,'y'=4,'x'=4,'c'=2,'g'=8] {'c','h','g'}, dimensions={0} | all-to-all | bytes 131072 | tf_op jit(solution)/shard_map/all_to_all | solution.py:209
  94.4 0.8 shard_map.43
Async XLA Ops:
  0.0 11.1 %copy-start = (f32[64,96]{1,0:T(8,128)S(1)}, f32[64,96]{1,0:T(8,128)}, u32[]{:S(2)}) copy-start(f32[64,96]{1,0:T(8,128)} %factor_ref.1) | copy-start | bytes 73732
  2.3 10.7 %collective-permute-start = (f32[4,48,1024]{2,1,0:T(8,128)S(1)}, f32[4,48,1024]{2,1,0:T(8,128)S(1)}, u32[]{:S(2)}, u32[]{:S(2)}) collective-permute-start(f32[4,48,1024]{2,1,0:T(8,128)S(1)} %get-tuple-element.14), channel_id=1, source_target_pairs={{0,8},{8,0},{1,9},{9,1},{2,10},{10,2},{3,11},{11,3},{4,12},{12,4},... | collective-permute-start | bytes 2359304 | tf_op jit(solution)/shard_map/ppermute | solution.py:203

commit v5 on v4

--- a/solution.py
+++ b/solution.py
@@ -21,19 +21,20 @@
     return lax.dot_general(left, right, (((1,), (1,)), ((), ())), preferred_element_type=F32)
 
 
-def halves(rows):
+def product(rows, field):
     top, low = split(rows)
     upper = jnp.concatenate([top, top], axis=1)
-    return jnp.concatenate([upper, jnp.concatenate([low, jnp.zeros_like(low)], axis=1)], axis=0)
-
-
-def product(left, right):
-    both = dot_nt(left, right)
+    left = jnp.concatenate([upper, jnp.concatenate([low, jnp.zeros_like(low)], axis=1)], axis=0)
+    top, low = split(field.reshape(1024, 128))
+    both = dot_nt(left, jnp.concatenate([top, low], axis=1))
     return both[0:48] + both[48:96]
 
 
-def others_kernel(species_hbm, factor_hbm, others_ref, right_ref, left_ref, field_ref, factor_ref, sems):
-    c = lax.axis_index("c")
+def rows_for(core, factor_ref):
+    return factor_ref[pl.ds(pl.multiple_of(48 * core, 48), 48)]
+
+
+def others_kernel(species_hbm, factor_hbm, others_ref, field_ref, factor_ref, sems):
     copies = [pltpu.make_async_copy(factor_hbm, factor_ref, sems.at[4])]
     for j in range(4):
         rows = pl.ds(16 * j, 16)
@@ -41,14 +42,10 @@
     for copy in copies:
         copy.start()
     copies[0].wait()
-    left_ref[...] = halves(factor_ref[pl.ds(pl.multiple_of(48 * c, 48), 48)])
-    left = halves(factor_ref[pl.ds(pl.multiple_of(48 * (1 - c), 48), 48)])
+    rows = rows_for(1 - lax.axis_index("c"), factor_ref)
     for j in range(4):
         copies[1 + j].wait()
-        top, low = split(field_ref[16 * j : 16 * j + 16].reshape(1024, 128))
-        right = jnp.concatenate([top, low], axis=1)
-        right_ref[j] = right
-        others_ref[j] = product(left, right)
+        others_ref[j] = product(rows, field_ref[16 * j : 16 * j + 16])
 
 
 def others_product(species, factor_y):
@@ -58,19 +55,15 @@
         in_specs=[hbm, hbm],
         out_shape=[
             jax.ShapeDtypeStruct((4, 48, 1024), F32),
-            pltpu.VMEM((4, 1024, 256), BF16),
-            pltpu.VMEM((96, 256), BF16),
-        ],
-        scratch_shapes=[
             pltpu.VMEM((64, 64, 128), F32),
             pltpu.VMEM((R, 128), F32),
-            pltpu.SemaphoreType.DMA((5,)),
         ],
+        scratch_shapes=[pltpu.SemaphoreType.DMA((5,))],
         compiler_params=PARAMS,
     )(pltpu.with_memory_space_constraint(species, pltpu.HBM), pltpu.with_memory_space_constraint(factor_y.T, pltpu.HBM))
 
 
-def early_kernel(left_ref, right_ref, factor_ref, out_ref, top_ref, low_ref, four_ref):
+def early_kernel(field_ref, factor_y_ref, factor_ref, out_ref, top_ref, low_ref, four_ref):
     four_ref[...] = jnp.zeros_like(four_ref)
     for q in range(4):
         four_ref[64 * q : 64 * q + 64, R * q : R * q + R] = factor_ref[...]
@@ -79,36 +72,40 @@
     @pl.when(lax.axis_index("c") == 1)
     def _():
         for j in range(4):
-            out_ref[j] = product(left_ref[...], right_ref[j])
-
-
-def early_product(left, right, factor_z):
+            out_ref[j] = product(rows_for(1, factor_y_ref), field_ref[16 * j : 16 * j + 16])
+
+
+def early_product(field, factor_y, factor_z):
     four = pltpu.VMEM((256, 384), BF16)
     return pl.pallas_call(
         early_kernel,
         out_shape=[pltpu.VMEM((4, 48, 1024), F32), four, four],
         scratch_shapes=[pltpu.VMEM((256, 384), F32)],
         compiler_params=PARAMS,
-    )(left, right, factor_z)
-
-
-def add_kernel(left_ref, right_ref, mine_ref, received_ref, out_ref):
+    )(field, factor_y, factor_z)
+
+
+def add_kernel(field_ref, factor_ref, mine_ref, received_ref, out_ref):
     c = lax.axis_index("c")
 
     @pl.when(c == 0)
     def _():
         for j in range(4):
-            out_ref[j] = product(left_ref[...], right_ref[j]) + received_ref[j]
+            field = field_ref[16 * j : 16 * j + 16].reshape(1024, 128)
+            own = lax.dot_general(
+                rows_for(0, factor_ref), field, (((1,), (1,)), ((), ())), precision=HIGHEST, preferred_element_type=F32
+            )
+            out_ref[j] = own + received_ref[j]
 
     @pl.when(c == 1)
     def _():
         out_ref[...] = mine_ref[...] + received_ref[...]
 
 
-def add(left, right, mine, received):
+def add(field, factor, mine, received):
     return pl.pallas_call(
         add_kernel, out_shape=pltpu.VMEM(mine.shape, F32), compiler_params=PARAMS
-    )(left, right, mine, received)
+    )(field, factor, mine, received)
 
 
 def z_kernel(parts_ref, factor_ref, rest_ref, out_ref):
@@ -198,9 +195,9 @@
 
 
 def body(species, factor_y, factor_z):
-    others, right, left = others_product(species, factor_y)
-    mine, factor, rest = early_product(left, right, factor_z)
-    along_y = add(left, right, mine, lax.ppermute(others, "c", [(0, 1), (1, 0)]))
+    others, field, factor_y = others_product(species, factor_y)
+    mine, factor, rest = early_product(field, factor_y, factor_z)
+    along_y = add(field, factor_y, mine, lax.ppermute(others, "c", [(0, 1), (1, 0)]))
     parts = z_product(lax.all_to_all(along_y, "x", 0, 0, tiled=True), factor, rest)
     parts = lax.all_to_all(parts.reshape(144, 4, 128), ("h", "g"), 0, 0, tiled=True)
     both = copies(parts.reshape(2, 8, 9, 4, 128)).reshape(144, 8, 128)

time: 95.5 us -> 93.2 us (0.976)
  blocking collectives: 80.3 us -> 78 us
    all_to_all x1, blocking collectives: 13.7 us -> 12.2 us  [body(): lax.all_to_all(along_y, 'x', 0, 0, tiled=True)]
where the time goes in v5:
time: 93.2 us; the launch traced here: 92.9 us
  blocking collectives  78 us (84%)
  starting transfers between devices  8.79 us (9%)
  Pallas kernels  5.08 us (5%)
  waiting for transfers between devices  0.99 us (1%)
    all_to_all x1, blocking collectives, body(): return last(lax.all_to_all(terms, ('c', 'h', 'g'), 0, 0, tiled=True))  28.5 us
    all_to_all x1, blocking collectives, body(): lax.all_to_all(parts.reshape(144, 4, 128), ('h', 'g'), 0, 0, tiled=True)  23.3 us
    all_to_all x1, blocking collectives, body(): both = lax.all_to_all(both, ('y', 'x'), 0, 0, tiled=True)  14.1 us
    all_to_all x1, blocking collectives, body(): lax.all_to_all(along_y, 'x', 0, 0, tiled=True)  12.2 us
    ppermute x1, starting transfers between devices, body(): lax.ppermute(others, 'c', [(0, 1), (1, 0)])  8.79 us
    pallas_call x1, Pallas kernels, others_product(): pl.pallas_call(others_kernel, in_specs=[hbm, hbm], out_shape=[jax.ShapeDt...  2.33 us
  transfers between devices with their start and end apart: 1, of which 1 were waited for; matrix products, arithmetic and copies ran while one was open for 0% of the time, Pallas kernels for 1%

profile of v5, /device:TPU:1, one launch (start us, length us, event | category | flops | bytes accessed | tf_op | source)
XLA Modules:
  0.0 92.9 jit_solution(15854550133994548092)
XLA Ops:
  0.0 0.0 copy-start
  0.0 2.3 %shard_map.37 = (f32[4,48,1024]{2,1,0:T(8,128)S(1)}, f32[64,64,128]{2,1,0:T(8,128)S(1)}, f32[96,128]{1,0:T(8,128)S(1)}) custom-call(f32[64,64,128]{2,1,0:T(8,128)} %species_hbm.1, f32[96,128]{1,0:T(8,128)} %bitcast.12), custom_call_target="tpu_custom_call" | custom-call | tf_op jit(solution)/shard_map/pallas_call | solution.py:53
  2.3 8.8 %collective-permute-start = (f32[4,48,1024]{2,1,0:T(8,128)S(1)}, f32[4,48,1024]{2,1,0:T(8,128)S(1)}, u32[]{:S(2)}, u32[]{:S(2)}) collective-permute-start(f32[4,48,1024]{2,1,0:T(8,128)S(1)} %get-tuple-element.14), channel_id=1, source_target_pairs={{0,8},{8,0},{1,9},{9,1},{2,10},{10,2},{3,11},{11,3},{4,12},{12,4},... | collective-permute-start | bytes 2359304 | tf_op jit(solution)/shard_map/ppermute | solution.py:200
  11.1 0.0 copy-done
  11.1 0.9 shard_map.38
  12.0 1.0 %collective-permute-done.received_ref = f32[4,48,1024]{2,1,0:T(8,128)S(1)} collective-permute-done((f32[4,48,1024]{2,1,0:T(8,128)S(1)}, f32[4,48,1024]{2,1,0:T(8,128)S(1)}, u32[]{:S(2)}, u32[]{:S(2)}) %collective-permute-start) | collective-permute-done | bytes 786464 | tf_op jit(solution)/shard_map/ppermute | solution.py:200
  13.0 0.1 shard_map.39
  13.1 12.2 %all_to_all.20.parts_ref = f32[4,48,1024]{2,1,0:T(8,128)S(1)} all-to-all(f32[4,48,1024]{2,1,0:T(8,128)S(1)} %shard_map.39), channel_id=1, replica_groups=mesh['h'=2,'y'=4,'x'=4,'c'=2,'g'=8] {'x'}, dimensions={0} | all-to-all | bytes 1572864 | tf_op jit(solution)/shard_map/all_to_all | solution.py:201
  25.3 0.3 shard_map.40
  25.6 23.3 %all_to_all.21 = f32[144,4,128]{2,1,0:T(4,128)S(1)} all-to-all(f32[144,4,128]{2,1,0:T(4,128)S(1)} %bitcast.10), channel_id=1, replica_groups=mesh['h'=2,'y'=4,'x'=4,'c'=2,'g'=8] {'h','g'}, dimensions={0} | all-to-all | bytes 589824 | tf_op jit(solution)/shard_map/all_to_all | solution.py:202
  48.9 0.1 shard_map.41
  49.0 14.1 %all_to_all.22 = f32[144,8,128]{2,1,0:T(8,128)S(1)} all-to-all(f32[144,8,128]{2,1,0:T(8,128)S(1)} %bitcast.7), channel_id=1, replica_groups=mesh['h'=2,'y'=4,'x'=4,'c'=2,'g'=8] {'y','x'}, dimensions={0} | all-to-all | bytes 1179648 | tf_op jit(solution)/shard_map/all_to_all | solution.py:204
  63.0 0.5 shard_map.42
  63.6 28.5 %all_to_all.23.terms_ref = f32[32,4,128]{2,1,0:T(4,128)S(1)} all-to-all(f32[32,4,128]{2,1,0:T(4,128)S(1)} %bitcast.11), channel_id=1, replica_groups=mesh['h'=2,'y'=4,'x'=4,'c'=2,'g'=8] {'c','h','g'}, dimensions={0} | all-to-all | bytes 131072 | tf_op jit(solution)/shard_map/all_to_all | solution.py:206
  92.1 0.8 shard_map.43
Async XLA Ops:
  0.0 11.1 %copy-start = (f32[64,96]{1,0:T(8,128)S(1)}, f32[64,96]{1,0:T(8,128)}, u32[]{:S(2)}) copy-start(f32[64,96]{1,0:T(8,128)} %factor_ref.1) | copy-start | bytes 73732
  2.3 10.7 %collective-permute-start = (f32[4,48,1024]{2,1,0:T(8,128)S(1)}, f32[4,48,1024]{2,1,0:T(8,128)S(1)}, u32[]{:S(2)}, u32[]{:S(2)}) collective-permute-start(f32[4,48,1024]{2,1,0:T(8,128)S(1)} %get-tuple-element.14), channel_id=1, source_target_pairs={{0,8},{8,0},{1,9},{9,1},{2,10},{10,2},{3,11},{11,3},{4,12},{12,4},... | collective-permute-start | bytes 2359304 | tf_op jit(solution)/shard_map/ppermute | solution.py:200

commit v6 on v5

--- a/solution.py
+++ b/solution.py
@@ -21,11 +21,14 @@
     return lax.dot_general(left, right, (((1,), (1,)), ((), ())), preferred_element_type=F32)
 
 
-def product(rows, field):
+def halves(rows):
     top, low = split(rows)
     upper = jnp.concatenate([top, top], axis=1)
-    left = jnp.concatenate([upper, jnp.concatenate([low, jnp.zeros_like(low)], axis=1)], axis=0)
-    top, low = split(field.reshape(1024, 128))
+    return jnp.concatenate([upper, jnp.concatenate([low, jnp.zeros_like(low)], axis=1)], axis=0)
+
+
+def product(left, field):
+    top, low = split(field.reshape(-1, 128))
     both = dot_nt(left, jnp.concatenate([top, low], axis=1))
     return both[0:48] + both[48:96]
 
@@ -35,17 +38,18 @@
 
 
 def others_kernel(species_hbm, factor_hbm, others_ref, field_ref, factor_ref, sems):
-    copies = [pltpu.make_async_copy(factor_hbm, factor_ref, sems.at[4])]
-    for j in range(4):
-        rows = pl.ds(16 * j, 16)
+    copies = [pltpu.make_async_copy(factor_hbm, factor_ref, sems.at[2])]
+    for j in range(2):
+        rows = pl.ds(32 * j, 32)
         copies.append(pltpu.make_async_copy(species_hbm.at[rows], field_ref.at[rows], sems.at[j]))
     for copy in copies:
         copy.start()
     copies[0].wait()
-    rows = rows_for(1 - lax.axis_index("c"), factor_ref)
+    left = halves(rows_for(1 - lax.axis_index("c"), factor_ref))
     for j in range(4):
-        copies[1 + j].wait()
-        others_ref[j] = product(rows, field_ref[16 * j : 16 * j + 16])
+        if j % 2 == 0:
+            copies[1 + j // 2].wait()
+        others_ref[j] = product(left, field_ref[16 * j : 16 * j + 16])
 
 
 def others_product(species, factor_y):
@@ -58,7 +62,7 @@
             pltpu.VMEM((64, 64, 128), F32),
             pltpu.VMEM((R, 128), F32),
         ],
-        scratch_shapes=[pltpu.SemaphoreType.DMA((5,))],
+        scratch_shapes=[pltpu.SemaphoreType.DMA((3,))],
         compiler_params=PARAMS,
     )(pltpu.with_memory_space_constraint(species, pltpu.HBM), pltpu.with_memory_space_constraint(factor_y.T, pltpu.HBM))
 
@@ -71,8 +75,9 @@
 
     @pl.when(lax.axis_index("c") == 1)
     def _():
+        left = halves(rows_for(1, factor_y_ref))
         for j in range(4):
-            out_ref[j] = product(rows_for(1, factor_y_ref), field_ref[16 * j : 16 * j + 16])
+            out_ref[j] = product(left, field_ref[16 * j : 16 * j + 16])
 
 
 def early_product(field, factor_y, factor_z):
@@ -156,7 +161,7 @@
         top, low = rows_of(8 * (x % 2), 8, i)
         right, rest = rows_of(4 * y, 4, i)
         total += dot_nt(top, right) + (dot_nt(low, right) + dot_nt(top, rest))
-    terms_ref[...] = total
+    terms_ref[0:256] = total
     first = (lax.broadcasted_iota(jnp.int32, (4, 128), 1) & 4) == 0
     for c in range(2):
         for k in range(4):
@@ -172,7 +177,7 @@
     return pl.pallas_call(
         gram_kernel,
         out_shape=jax.ShapeDtypeStruct((2, 2, 8, 4, 128), F32),
-        scratch_shapes=[pltpu.VMEM((256, 128), F32)],
+        scratch_shapes=[pltpu.VMEM((320, 128), F32)],
         compiler_params=PARAMS,
     )(both)
 

time: 93.2 us -> 93.1 us (level)
  no operation moved by 1% of the time
where the time goes in v6:
time: 93.1 us; the launch traced here: 92.8 us
  blocking collectives  78 us (84%)
  starting transfers between devices  8.79 us (9%)
  Pallas kernels  4.97 us (5%)
  waiting for transfers between devices  0.99 us (1%)
    all_to_all x1, blocking collectives, body(): return last(lax.all_to_all(terms, ('c', 'h', 'g'), 0, 0, tiled=True))  28.5 us
    all_to_all x1, blocking collectives, body(): lax.all_to_all(parts.reshape(144, 4, 128), ('h', 'g'), 0, 0, tiled=True)  23.3 us
    all_to_all x1, blocking collectives, body(): both = lax.all_to_all(both, ('y', 'x'), 0, 0, tiled=True)  14.1 us
    all_to_all x1, blocking collectives, body(): lax.all_to_all(along_y, 'x', 0, 0, tiled=True)  12.2 us
    ppermute x1, starting transfers between devices, body(): lax.ppermute(others, 'c', [(0, 1), (1, 0)])  8.79 us
    pallas_call x1, Pallas kernels, others_product(): pl.pallas_call(others_kernel, in_specs=[hbm, hbm], out_shape=[jax.ShapeDt...  2.21 us
  transfers between devices with their start and end apart: 1, of which 1 were waited for; matrix products, arithmetic and copies ran while one was open for 0% of the time, Pallas kernels for 1%

profile of v6, /device:TPU:1, one launch (start us, length us, event | category | flops | bytes accessed | tf_op | source)
XLA Modules:
  0.0 92.8 jit_solution(11359980970547084313)
XLA Ops:
  0.0 0.0 copy-start
  0.0 2.2 %shard_map.37 = (f32[4,48,1024]{2,1,0:T(8,128)S(1)}, f32[64,64,128]{2,1,0:T(8,128)S(1)}, f32[96,128]{1,0:T(8,128)S(1)}) custom-call(f32[64,64,128]{2,1,0:T(8,128)} %species_hbm.1, f32[96,128]{1,0:T(8,128)} %bitcast.12), custom_call_target="tpu_custom_call" | custom-call | tf_op jit(solution)/shard_map/pallas_call | solution.py:57
  2.2 8.8 %collective-permute-start = (f32[4,48,1024]{2,1,0:T(8,128)S(1)}, f32[4,48,1024]{2,1,0:T(8,128)S(1)}, u32[]{:S(2)}, u32[]{:S(2)}) collective-permute-start(f32[4,48,1024]{2,1,0:T(8,128)S(1)} %get-tuple-element.14), channel_id=1, source_target_pairs={{0,8},{8,0},{1,9},{9,1},{2,10},{10,2},{3,11},{11,3},{4,12},{12,4},... | collective-permute-start | bytes 2359304 | tf_op jit(solution)/shard_map/ppermute | solution.py:205
  11.0 0.0 copy-done
  11.0 0.9 shard_map.38
  11.9 1.0 %collective-permute-done.received_ref = f32[4,48,1024]{2,1,0:T(8,128)S(1)} collective-permute-done((f32[4,48,1024]{2,1,0:T(8,128)S(1)}, f32[4,48,1024]{2,1,0:T(8,128)S(1)}, u32[]{:S(2)}, u32[]{:S(2)}) %collective-permute-start) | collective-permute-done | bytes 786464 | tf_op jit(solution)/shard_map/ppermute | solution.py:205
  12.9 0.1 shard_map.39
  13.0 12.2 %all_to_all.20.parts_ref = f32[4,48,1024]{2,1,0:T(8,128)S(1)} all-to-all(f32[4,48,1024]{2,1,0:T(8,128)S(1)} %shard_map.39), channel_id=1, replica_groups=mesh['h'=2,'y'=4,'x'=4,'c'=2,'g'=8] {'x'}, dimensions={0} | all-to-all | bytes 1572864 | tf_op jit(solution)/shard_map/all_to_all | solution.py:206
  25.2 0.3 shard_map.40
  25.5 23.3 %all_to_all.21 = f32[144,4,128]{2,1,0:T(4,128)S(1)} all-to-all(f32[144,4,128]{2,1,0:T(4,128)S(1)} %bitcast.10), channel_id=1, replica_groups=mesh['h'=2,'y'=4,'x'=4,'c'=2,'g'=8] {'h','g'}, dimensions={0} | all-to-all | bytes 589824 | tf_op jit(solution)/shard_map/all_to_all | solution.py:207
  48.8 0.1 shard_map.41
  48.9 14.1 %all_to_all.22 = f32[144,8,128]{2,1,0:T(8,128)S(1)} all-to-all(f32[144,8,128]{2,1,0:T(8,128)S(1)} %bitcast.7), channel_id=1, replica_groups=mesh['h'=2,'y'=4,'x'=4,'c'=2,'g'=8] {'y','x'}, dimensions={0} | all-to-all | bytes 1179648 | tf_op jit(solution)/shard_map/all_to_all | solution.py:209
  62.9 0.5 shard_map.42
  63.5 28.5 %all_to_all.23.terms_ref = f32[32,4,128]{2,1,0:T(4,128)S(1)} all-to-all(f32[32,4,128]{2,1,0:T(4,128)S(1)} %bitcast.11), channel_id=1, replica_groups=mesh['h'=2,'y'=4,'x'=4,'c'=2,'g'=8] {'c','h','g'}, dimensions={0} | all-to-all | bytes 131072 | tf_op jit(solution)/shard_map/all_to_all | solution.py:211
  91.9 0.8 shard_map.43
Async XLA Ops:
  0.0 11.0 %copy-start = (f32[64,96]{1,0:T(8,128)S(1)}, f32[64,96]{1,0:T(8,128)}, u32[]{:S(2)}) copy-start(f32[64,96]{1,0:T(8,128)} %factor_ref.1) | copy-start | bytes 73732
  2.2 10.7 %collective-permute-start = (f32[4,48,1024]{2,1,0:T(8,128)S(1)}, f32[4,48,1024]{2,1,0:T(8,128)S(1)}, u32[]{:S(2)}, u32[]{:S(2)}) collective-permute-start(f32[4,48,1024]{2,1,0:T(8,128)S(1)} %get-tuple-element.14), channel_id=1, source_target_pairs={{0,8},{8,0},{1,9},{9,1},{2,10},{10,2},{3,11},{11,3},{4,12},{12,4},... | collective-permute-start | bytes 2359304 | tf_op jit(solution)/shard_map/ppermute | solution.py:205

commit v7 on v6

--- a/solution.py
+++ b/solution.py
@@ -67,38 +67,52 @@
     )(pltpu.with_memory_space_constraint(species, pltpu.HBM), pltpu.with_memory_space_constraint(factor_y.T, pltpu.HBM))
 
 
-def early_kernel(field_ref, factor_y_ref, factor_ref, out_ref, top_ref, low_ref, four_ref):
+def set_up(factor_ref, top_ref, low_ref, pick_ref, four_ref):
     four_ref[...] = jnp.zeros_like(four_ref)
     for q in range(4):
         four_ref[64 * q : 64 * q + 64, R * q : R * q + R] = factor_ref[...]
     top_ref[...], low_ref[...] = split(four_ref[...])
-
+    row = lax.broadcasted_iota(jnp.int32, (128, 128), 0)
+    lane = lax.broadcasted_iota(jnp.int32, (128, 128), 1)
+    source = (row & 3) * 32 + ((row >> 4) & 3) * 8 + (row >> 6) * 4 + ((row >> 2) & 3)
+    pick_ref[...] = jnp.where(lane == source, 1.0, 0.0).astype(F32)
+
+
+FOUR = pltpu.VMEM((256, 384), BF16)
+PICK = pltpu.VMEM((128, 128), F32)
+HALF = pltpu.VMEM((4, 48, 1024), F32)
+
+
+def early_kernel(field_ref, factor_y_ref, factor_ref, out_ref, top_ref, low_ref, pick_ref, four_ref):
     @pl.when(lax.axis_index("c") == 1)
     def _():
+        set_up(factor_ref, top_ref, low_ref, pick_ref, four_ref)
         left = halves(rows_for(1, factor_y_ref))
         for j in range(4):
             out_ref[j] = product(left, field_ref[16 * j : 16 * j + 16])
 
 
 def early_product(field, factor_y, factor_z):
-    four = pltpu.VMEM((256, 384), BF16)
     return pl.pallas_call(
         early_kernel,
-        out_shape=[pltpu.VMEM((4, 48, 1024), F32), four, four],
+        out_shape=[HALF, FOUR, FOUR, PICK],
         scratch_shapes=[pltpu.VMEM((256, 384), F32)],
         compiler_params=PARAMS,
     )(field, factor_y, factor_z)
 
 
-def add_kernel(field_ref, factor_ref, mine_ref, received_ref, out_ref):
+def add_kernel(
+    field_ref, factor_y_ref, factor_ref, received_ref, mine_ref, top_in, low_in, pick_in, out_ref, top_ref, low_ref, pick_ref, four_ref
+):
     c = lax.axis_index("c")
 
     @pl.when(c == 0)
     def _():
+        set_up(factor_ref, top_ref, low_ref, pick_ref, four_ref)
         for j in range(4):
             field = field_ref[16 * j : 16 * j + 16].reshape(1024, 128)
             own = lax.dot_general(
-                rows_for(0, factor_ref), field, (((1,), (1,)), ((), ())), precision=HIGHEST, preferred_element_type=F32
+                rows_for(0, factor_y_ref), field, (((1,), (1,)), ((), ())), precision=HIGHEST, preferred_element_type=F32
             )
             out_ref[j] = own + received_ref[j]
 
@@ -107,10 +121,14 @@
         out_ref[...] = mine_ref[...] + received_ref[...]
 
 
-def add(field, factor, mine, received):
-    return pl.pallas_call(
-        add_kernel, out_shape=pltpu.VMEM(mine.shape, F32), compiler_params=PARAMS
-    )(field, factor, mine, received)
+def add(field, factor_y, factor_z, received, early):
+    return pl.pallas_call(
+        add_kernel,
+        out_shape=[HALF, FOUR, FOUR, PICK],
+        scratch_shapes=[pltpu.VMEM((256, 384), F32)],
+        input_output_aliases={5: 1, 6: 2, 7: 3},
+        compiler_params=PARAMS,
+    )(field, factor_y, factor_z, received, *early)
 
 
 def z_kernel(parts_ref, factor_ref, rest_ref, out_ref):
@@ -134,7 +152,7 @@
 
 def copies_kernel(parts_ref, out_ref, both_ref):
     for h in range(2):
-        both_ref[:, 4 * h : 4 * h + 4] = parts_ref[h].sum(0)
+        both_ref[:, 4 * h : 4 * h + 4] = parts_ref[:, h].sum(0)
     for n in range(16):
         out_ref[n] = both_ref[...]
 
@@ -169,46 +187,46 @@
                 start = 32 * c + 8 * k + t + 4 * (x // 2)
                 even = terms_ref[pl.ds(start, 4, stride=64), :]
                 odd = terms_ref[pl.ds(start + 1, 4, stride=64), :]
-                out_ref[c, 0, 2 * k + t // 2] = jnp.where(first, even, pltpu.roll(odd, 4, 1))
-                out_ref[c, 1, 2 * k + t // 2] = jnp.where(first, pltpu.roll(even, 124, 1), odd)
+                out_ref[2 * k + t // 2, 0, c] = jnp.where(first, even, pltpu.roll(odd, 4, 1))
+                out_ref[2 * k + t // 2, 1, c] = jnp.where(first, pltpu.roll(even, 124, 1), odd)
 
 
 def gram_terms(both):
     return pl.pallas_call(
         gram_kernel,
-        out_shape=jax.ShapeDtypeStruct((2, 2, 8, 4, 128), F32),
+        out_shape=jax.ShapeDtypeStruct((8, 2, 2, 4, 128), F32),
         scratch_shapes=[pltpu.VMEM((320, 128), F32)],
         compiler_params=PARAMS,
     )(both)
 
 
-def last_kernel(terms_ref, out_ref):
+def last_kernel(terms_ref, pick_ref, out_ref):
     total = terms_ref[...].sum(0)
-    row = lax.broadcasted_iota(jnp.int32, (64, 128), 0)
-    lane = lax.broadcasted_iota(jnp.int32, (64, 128), 1)
-    source = (row & 3) * 32 + (row >> 4) * 8 + ((row >> 2) & 3)
-    for half in range(2):
-        pick = jnp.where(lane == source + 4 * half, 1.0, 0.0).astype(F32)
-        moved = lax.dot_general(total, pick, (((1,), (1,)), ((), ())), precision=HIGHEST, preferred_element_type=F32)
-        out_ref[4 * half : 4 * half + 4] = moved / (R * R)
-
-
-def last(terms):
+    moved = lax.dot_general(
+        total, pick_ref[...], (((1,), (1,)), ((), ())), precision=HIGHEST, preferred_element_type=F32
+    ) / (R * R)
+    out_ref[0:4] = moved[:, 0:64]
+    out_ref[4:8] = moved[:, 64:128]
+
+
+def last(terms, pick):
     return pl.pallas_call(
         last_kernel, out_shape=jax.ShapeDtypeStruct((8, 64), F32), compiler_params=PARAMS
-    )(terms).T
+    )(terms, pick).T
 
 
 def body(species, factor_y, factor_z):
     others, field, factor_y = others_product(species, factor_y)
-    mine, factor, rest = early_product(field, factor_y, factor_z)
-    along_y = add(field, factor_y, mine, lax.ppermute(others, "c", [(0, 1), (1, 0)]))
+    early = early_product(field, factor_y, factor_z)
+    along_y, factor, rest, pick = add(
+        field, factor_y, factor_z, lax.ppermute(others, "c", [(0, 1), (1, 0)]), early
+    )
     parts = z_product(lax.all_to_all(along_y, "x", 0, 0, tiled=True), factor, rest)
-    parts = lax.all_to_all(parts.reshape(144, 4, 128), ("h", "g"), 0, 0, tiled=True)
-    both = copies(parts.reshape(2, 8, 9, 4, 128)).reshape(144, 8, 128)
+    parts = lax.all_to_all(parts.reshape(144, 4, 128), ("g", "h"), 0, 0, tiled=True)
+    both = copies(parts.reshape(8, 2, 9, 4, 128)).reshape(144, 8, 128)
     both = lax.all_to_all(both, ("y", "x"), 0, 0, tiled=True)
     terms = gram_terms(both.reshape(16, 9, 8, 128)).reshape(32, 4, 128)
-    return last(lax.all_to_all(terms, ("c", "h", "g"), 0, 0, tiled=True))
+    return last(lax.all_to_all(terms, ("g", "h", "c"), 0, 0, tiled=True), pick)
 
 
 def solution(mesh):

time: 93.1 us -> 92.5 us (level)
  no operation moved by 1% of the time
where the time goes in v7:
time: 92.5 us; the launch traced here: 92.2 us
  blocking collectives  77.4 us (84%)
  starting transfers between devices  8.79 us (10%)
  Pallas kernels  4.94 us (5%)
  waiting for transfers between devices  1.07 us (1%)
    all_to_all x1, blocking collectives, body(): return last(lax.all_to_all(terms, ('g', 'h', 'c'), 0, 0, tiled=True), pick)  25.8 us
    all_to_all x1, blocking collectives, body(): lax.all_to_all(parts.reshape(144, 4, 128), ('g', 'h'), 0, 0, tiled=True)  25.4 us
    all_to_all x1, blocking collectives, body(): both = lax.all_to_all(both, ('y', 'x'), 0, 0, tiled=True)  14.1 us
    all_to_all x1, blocking collectives, body(): lax.all_to_all(along_y, 'x', 0, 0, tiled=True)  12.2 us
    ppermute x1, starting transfers between devices, body(): lax.ppermute(others, 'c', [(0, 1), (1, 0)])  8.79 us
    pallas_call x1, Pallas kernels, others_product(): pl.pallas_call(others_kernel, in_specs=[hbm, hbm], out_shape=[jax.ShapeDt...  2.21 us
  transfers between devices with their start and end apart: 1, of which 1 were waited for; matrix products, arithmetic and copies ran while one was open for 0% of the time, Pallas kernels for 1%

profile of v7, /device:TPU:1, one launch (start us, length us, event | category | flops | bytes accessed | tf_op | source)
XLA Modules:
  0.0 92.2 jit_solution(17601223781181253206)
XLA Ops:
  0.0 0.0 copy-start
  0.0 2.2 %shard_map.37 = (f32[4,48,1024]{2,1,0:T(8,128)S(1)}, f32[64,64,128]{2,1,0:T(8,128)S(1)}, f32[96,128]{1,0:T(8,128)S(1)}) custom-call(f32[64,64,128]{2,1,0:T(8,128)} %species_hbm.1, f32[96,128]{1,0:T(8,128)} %bitcast.12), custom_call_target="tpu_custom_call" | custom-call | tf_op jit(solution)/shard_map/pallas_call | solution.py:57
  2.2 8.8 %collective-permute-start = (f32[4,48,1024]{2,1,0:T(8,128)S(1)}, f32[4,48,1024]{2,1,0:T(8,128)S(1)}, u32[]{:S(2)}, u32[]{:S(2)}) collective-permute-start(f32[4,48,1024]{2,1,0:T(8,128)S(1)} %get-tuple-element.18), channel_id=1, source_target_pairs={{0,8},{8,0},{1,9},{9,1},{2,10},{10,2},{3,11},{11,3},{4,12},{12,4},... | collective-permute-start | bytes 2359304 | tf_op jit(solution)/shard_map/ppermute | solution.py:222
  11.0 0.0 copy-done
  11.0 0.8 shard_map.38
  11.8 1.1 %collective-permute-done.received_ref = f32[4,48,1024]{2,1,0:T(8,128)S(1)} collective-permute-done((f32[4,48,1024]{2,1,0:T(8,128)S(1)}, f32[4,48,1024]{2,1,0:T(8,128)S(1)}, u32[]{:S(2)}, u32[]{:S(2)}) %collective-permute-start) | collective-permute-done | bytes 786464 | tf_op jit(solution)/shard_map/ppermute | solution.py:222
  12.9 0.1 shard_map.39
  13.0 12.2 %all_to_all.20.parts_ref = f32[4,48,1024]{2,1,0:T(8,128)S(1)} all-to-all(f32[4,48,1024]{2,1,0:T(8,128)S(1)} %get-tuple-element.23), channel_id=1, replica_groups=mesh['h'=2,'y'=4,'x'=4,'c'=2,'g'=8] {'x'}, dimensions={0} | all-to-all | bytes 1572864 | tf_op jit(solution)/shard_map/all_to_all | solution.py:224
  25.2 0.3 shard_map.40
  25.5 25.4 %all_to_all.21 = f32[144,4,128]{2,1,0:T(4,128)S(1)} all-to-all(f32[144,4,128]{2,1,0:T(4,128)S(1)} %bitcast.10), channel_id=1, replica_groups=mesh['h'=2,'y'=4,'x'=4,'c'=2,'g'=8] {'g','h'}, dimensions={0} | all-to-all | bytes 589824 | tf_op jit(solution)/shard_map/all_to_all | solution.py:225
  50.9 0.1 shard_map.41
  51.0 14.1 %all_to_all.22 = f32[144,8,128]{2,1,0:T(8,128)S(1)} all-to-all(f32[144,8,128]{2,1,0:T(8,128)S(1)} %bitcast.7), channel_id=1, replica_groups=mesh['h'=2,'y'=4,'x'=4,'c'=2,'g'=8] {'y','x'}, dimensions={0} | all-to-all | bytes 1179648 | tf_op jit(solution)/shard_map/all_to_all | solution.py:227
  65.0 0.5 shard_map.42
  65.6 25.8 %all_to_all.23.terms_ref = f32[32,4,128]{2,1,0:T(4,128)S(1)} all-to-all(f32[32,4,128]{2,1,0:T(4,128)S(1)} %bitcast.11), channel_id=1, replica_groups=mesh['h'=2,'y'=4,'x'=4,'c'=2,'g'=8] {'g','h','c'}, dimensions={0} | all-to-all | bytes 131072 | tf_op jit(solution)/shard_map/all_to_all | solution.py:229
  91.4 0.9 shard_map.43
Async XLA Ops:
  0.0 11.0 %copy-start = (f32[64,96]{1,0:T(8,128)S(1)}, f32[64,96]{1,0:T(8,128)}, u32[]{:S(2)}) copy-start(f32[64,96]{1,0:T(8,128)} %factor_ref.3) | copy-start | bytes 73732
  2.2 10.7 %collective-permute-start = (f32[4,48,1024]{2,1,0:T(8,128)S(1)}, f32[4,48,1024]{2,1,0:T(8,128)S(1)}, u32[]{:S(2)}, u32[]{:S(2)}) collective-permute-start(f32[4,48,1024]{2,1,0:T(8,128)S(1)} %get-tuple-element.18), channel_id=1, source_target_pairs={{0,8},{8,0},{1,9},{9,1},{2,10},{10,2},{3,11},{11,3},{4,12},{12,4},... | collective-permute-start | bytes 2359304 | tf_op jit(solution)/shard_map/ppermute | solution.py:222

commit v8 on v7

--- a/solution.py
+++ b/solution.py
@@ -187,8 +187,8 @@
                 start = 32 * c + 8 * k + t + 4 * (x // 2)
                 even = terms_ref[pl.ds(start, 4, stride=64), :]
                 odd = terms_ref[pl.ds(start + 1, 4, stride=64), :]
-                out_ref[2 * k + t // 2, 0, c] = jnp.where(first, even, pltpu.roll(odd, 4, 1))
-                out_ref[2 * k + t // 2, 1, c] = jnp.where(first, pltpu.roll(even, 124, 1), odd)
+                out_ref[2 * k + t // 2, c, 0] = jnp.where(first, even, pltpu.roll(odd, 4, 1))
+                out_ref[2 * k + t // 2, c, 1] = jnp.where(first, pltpu.roll(even, 124, 1), odd)
 
 
 def gram_terms(both):
@@ -226,7 +226,7 @@
     both = copies(parts.reshape(8, 2, 9, 4, 128)).reshape(144, 8, 128)
     both = lax.all_to_all(both, ("y", "x"), 0, 0, tiled=True)
     terms = gram_terms(both.reshape(16, 9, 8, 128)).reshape(32, 4, 128)
-    return last(lax.all_to_all(terms, ("g", "h", "c"), 0, 0, tiled=True), pick)
+    return last(lax.all_to_all(terms, ("g", "c", "h"), 0, 0, tiled=True), pick)
 
 
 def solution(mesh):

time: 92.5 us -> 92 us (level)
  no operation moved by 1% of the time
where the time goes in v8:
time: 92 us; the launch traced here: 91.7 us
  blocking collectives  76.9 us (84%)
  starting transfers between devices  8.79 us (10%)
  Pallas kernels  4.94 us (5%)
  waiting for transfers between devices  1.07 us (1%)
    all_to_all x1, blocking collectives, body(): lax.all_to_all(parts.reshape(144, 4, 128), ('g', 'h'), 0, 0, tiled=True)  25.4 us
    all_to_all x1, blocking collectives, body(): return last(lax.all_to_all(terms, ('g', 'c', 'h'), 0, 0, tiled=True), pick)  25.3 us
    all_to_all x1, blocking collectives, body(): both = lax.all_to_all(both, ('y', 'x'), 0, 0, tiled=True)  14.1 us
    all_to_all x1, blocking collectives, body(): lax.all_to_all(along_y, 'x', 0, 0, tiled=True)  12.2 us
    ppermute x1, starting transfers between devices, body(): lax.ppermute(others, 'c', [(0, 1), (1, 0)])  8.79 us
    pallas_call x1, Pallas kernels, others_product(): pl.pallas_call(others_kernel, in_specs=[hbm, hbm], out_shape=[jax.ShapeDt...  2.21 us
  transfers between devices with their start and end apart: 1, of which 1 were waited for; matrix products, arithmetic and copies ran while one was open for 0% of the time, Pallas kernels for 1%

profile of v8, /device:TPU:1, one launch (start us, length us, event | category | flops | bytes accessed | tf_op | source)
XLA Modules:
  0.0 91.7 jit_solution(590873487414412032)
XLA Ops:
  0.0 0.0 copy-start
  0.0 2.2 %shard_map.37 = (f32[4,48,1024]{2,1,0:T(8,128)S(1)}, f32[64,64,128]{2,1,0:T(8,128)S(1)}, f32[96,128]{1,0:T(8,128)S(1)}) custom-call(f32[64,64,128]{2,1,0:T(8,128)} %species_hbm.1, f32[96,128]{1,0:T(8,128)} %bitcast.12), custom_call_target="tpu_custom_call" | custom-call | tf_op jit(solution)/shard_map/pallas_call | solution.py:57
  2.2 8.8 %collective-permute-start = (f32[4,48,1024]{2,1,0:T(8,128)S(1)}, f32[4,48,1024]{2,1,0:T(8,128)S(1)}, u32[]{:S(2)}, u32[]{:S(2)}) collective-permute-start(f32[4,48,1024]{2,1,0:T(8,128)S(1)} %get-tuple-element.18), channel_id=1, source_target_pairs={{0,8},{8,0},{1,9},{9,1},{2,10},{10,2},{3,11},{11,3},{4,12},{12,4},... | collective-permute-start | bytes 2359304 | tf_op jit(solution)/shard_map/ppermute | solution.py:222
  11.0 0.0 copy-done
  11.0 0.8 shard_map.38
  11.8 1.1 %collective-permute-done.received_ref = f32[4,48,1024]{2,1,0:T(8,128)S(1)} collective-permute-done((f32[4,48,1024]{2,1,0:T(8,128)S(1)}, f32[4,48,1024]{2,1,0:T(8,128)S(1)}, u32[]{:S(2)}, u32[]{:S(2)}) %collective-permute-start) | collective-permute-done | bytes 786464 | tf_op jit(solution)/shard_map/ppermute | solution.py:222
  12.9 0.1 shard_map.39
  13.0 12.2 %all_to_all.20.parts_ref = f32[4,48,1024]{2,1,0:T(8,128)S(1)} all-to-all(f32[4,48,1024]{2,1,0:T(8,128)S(1)} %get-tuple-element.23), channel_id=1, replica_groups=mesh['h'=2,'y'=4,'x'=4,'c'=2,'g'=8] {'x'}, dimensions={0} | all-to-all | bytes 1572864 | tf_op jit(solution)/shard_map/all_to_all | solution.py:224
  25.2 0.3 shard_map.40
  25.5 25.4 %all_to_all.21 = f32[144,4,128]{2,1,0:T(4,128)S(1)} all-to-all(f32[144,4,128]{2,1,0:T(4,128)S(1)} %bitcast.10), channel_id=1, replica_groups=mesh['h'=2,'y'=4,'x'=4,'c'=2,'g'=8] {'g','h'}, dimensions={0} | all-to-all | bytes 589824 | tf_op jit(solution)/shard_map/all_to_all | solution.py:225
  50.9 0.1 shard_map.41
  51.0 14.1 %all_to_all.22 = f32[144,8,128]{2,1,0:T(8,128)S(1)} all-to-all(f32[144,8,128]{2,1,0:T(8,128)S(1)} %bitcast.7), channel_id=1, replica_groups=mesh['h'=2,'y'=4,'x'=4,'c'=2,'g'=8] {'y','x'}, dimensions={0} | all-to-all | bytes 1179648 | tf_op jit(solution)/shard_map/all_to_all | solution.py:227
  65.0 0.5 shard_map.42
  65.6 25.3 %all_to_all.23.terms_ref = f32[32,4,128]{2,1,0:T(4,128)S(1)} all-to-all(f32[32,4,128]{2,1,0:T(4,128)S(1)} %bitcast.11), channel_id=1, replica_groups=mesh['h'=2,'y'=4,'x'=4,'c'=2,'g'=8] {'g','c','h'}, dimensions={0} | all-to-all | bytes 131072 | tf_op jit(solution)/shard_map/all_to_all | solution.py:229
  90.8 0.9 shard_map.43
Async XLA Ops:
  0.0 11.0 %copy-start = (f32[64,96]{1,0:T(8,128)S(1)}, f32[64,96]{1,0:T(8,128)}, u32[]{:S(2)}) copy-start(f32[64,96]{1,0:T(8,128)} %factor_ref.3) | copy-start | bytes 73732
  2.2 10.7 %collective-permute-start = (f32[4,48,1024]{2,1,0:T(8,128)S(1)}, f32[4,48,1024]{2,1,0:T(8,128)S(1)}, u32[]{:S(2)}, u32[]{:S(2)}) collective-permute-start(f32[4,48,1024]{2,1,0:T(8,128)S(1)} %get-tuple-element.18), channel_id=1, source_target_pairs={{0,8},{8,0},{1,9},{9,1},{2,10},{10,2},{3,11},{11,3},{4,12},{12,4},... | collective-permute-start | bytes 2359304 | tf_op jit(solution)/shard_map/ppermute | solution.py:222

commit v9 on v8

--- a/solution.py
+++ b/solution.py
@@ -187,14 +187,14 @@
                 start = 32 * c + 8 * k + t + 4 * (x // 2)
                 even = terms_ref[pl.ds(start, 4, stride=64), :]
                 odd = terms_ref[pl.ds(start + 1, 4, stride=64), :]
-                out_ref[2 * k + t // 2, c, 0] = jnp.where(first, even, pltpu.roll(odd, 4, 1))
-                out_ref[2 * k + t // 2, c, 1] = jnp.where(first, pltpu.roll(even, 124, 1), odd)
+                out_ref[0, c, 2 * k + t // 2] = jnp.where(first, even, pltpu.roll(odd, 4, 1))
+                out_ref[1, c, 2 * k + t // 2] = jnp.where(first, pltpu.roll(even, 124, 1), odd)
 
 
 def gram_terms(both):
     return pl.pallas_call(
         gram_kernel,
-        out_shape=jax.ShapeDtypeStruct((8, 2, 2, 4, 128), F32),
+        out_shape=jax.ShapeDtypeStruct((2, 2, 8, 4, 128), F32),
         scratch_shapes=[pltpu.VMEM((320, 128), F32)],
         compiler_params=PARAMS,
     )(both)
@@ -226,7 +226,7 @@
     both = copies(parts.reshape(8, 2, 9, 4, 128)).reshape(144, 8, 128)
     both = lax.all_to_all(both, ("y", "x"), 0, 0, tiled=True)
     terms = gram_terms(both.reshape(16, 9, 8, 128)).reshape(32, 4, 128)
-    return last(lax.all_to_all(terms, ("g", "c", "h"), 0, 0, tiled=True), pick)
+    return last(lax.all_to_all(terms, ("h", "c", "g"), 0, 0, tiled=True), pick)
 
 
 def solution(mesh):

time: 92 us -> 92.3 us (level)
  no operation moved by 1% of the time
where the time goes in v9:
time: 92.3 us; the launch traced here: 92 us
  blocking collectives  77.1 us (84%)
  starting transfers between devices  8.79 us (10%)
  Pallas kernels  4.94 us (5%)
  waiting for transfers between devices  1.07 us (1%)
    all_to_all x1, blocking collectives, body(): return last(lax.all_to_all(terms, ('h', 'c', 'g'), 0, 0, tiled=True), pick)  25.5 us
    all_to_all x1, blocking collectives, body(): lax.all_to_all(parts.reshape(144, 4, 128), ('g', 'h'), 0, 0, tiled=True)  25.4 us
    all_to_all x1, blocking collectives, body(): both = lax.all_to_all(both, ('y', 'x'), 0, 0, tiled=True)  14.1 us
    all_to_all x1, blocking collectives, body(): lax.all_to_all(along_y, 'x', 0, 0, tiled=True)  12.2 us
    ppermute x1, starting transfers between devices, body(): lax.ppermute(others, 'c', [(0, 1), (1, 0)])  8.79 us
    pallas_call x1, Pallas kernels, others_product(): pl.pallas_call(others_kernel, in_specs=[hbm, hbm], out_shape=[jax.ShapeDt...  2.21 us
  transfers between devices with their start and end apart: 1, of which 1 were waited for; matrix products, arithmetic and copies ran while one was open for 0% of the time, Pallas kernels for 1%

profile of v9, /device:TPU:1, one launch (start us, length us, event | category | flops | bytes accessed | tf_op | source)
XLA Modules:
  0.0 92.0 jit_solution(413846188245187110)
XLA Ops:
  0.0 0.0 copy-start
  0.0 2.2 %shard_map.37 = (f32[4,48,1024]{2,1,0:T(8,128)S(1)}, f32[64,64,128]{2,1,0:T(8,128)S(1)}, f32[96,128]{1,0:T(8,128)S(1)}) custom-call(f32[64,64,128]{2,1,0:T(8,128)} %species_hbm.1, f32[96,128]{1,0:T(8,128)} %bitcast.12), custom_call_target="tpu_custom_call" | custom-call | tf_op jit(solution)/shard_map/pallas_call | solution.py:57
  2.2 8.8 %collective-permute-start = (f32[4,48,1024]{2,1,0:T(8,128)S(1)}, f32[4,48,1024]{2,1,0:T(8,128)S(1)}, u32[]{:S(2)}, u32[]{:S(2)}) collective-permute-start(f32[4,48,1024]{2,1,0:T(8,128)S(1)} %get-tuple-element.18), channel_id=1, source_target_pairs={{0,8},{8,0},{1,9},{9,1},{2,10},{10,2},{3,11},{11,3},{4,12},{12,4},... | collective-permute-start | bytes 2359304 | tf_op jit(solution)/shard_map/ppermute | solution.py:222
  11.0 0.0 copy-done
  11.0 0.8 shard_map.38
  11.8 1.1 %collective-permute-done.received_ref = f32[4,48,1024]{2,1,0:T(8,128)S(1)} collective-permute-done((f32[4,48,1024]{2,1,0:T(8,128)S(1)}, f32[4,48,1024]{2,1,0:T(8,128)S(1)}, u32[]{:S(2)}, u32[]{:S(2)}) %collective-permute-start) | collective-permute-done | bytes 786464 | tf_op jit(solution)/shard_map/ppermute | solution.py:222
  12.9 0.1 shard_map.39
  13.0 12.2 %all_to_all.20.parts_ref = f32[4,48,1024]{2,1,0:T(8,128)S(1)} all-to-all(f32[4,48,1024]{2,1,0:T(8,128)S(1)} %get-tuple-element.23), channel_id=1, replica_groups=mesh['h'=2,'y'=4,'x'=4,'c'=2,'g'=8] {'x'}, dimensions={0} | all-to-all | bytes 1572864 | tf_op jit(solution)/shard_map/all_to_all | solution.py:224
  25.2 0.3 shard_map.40
  25.5 25.4 %all_to_all.21 = f32[144,4,128]{2,1,0:T(4,128)S(1)} all-to-all(f32[144,4,128]{2,1,0:T(4,128)S(1)} %bitcast.10), channel_id=1, replica_groups=mesh['h'=2,'y'=4,'x'=4,'c'=2,'g'=8] {'g','h'}, dimensions={0} | all-to-all | bytes 589824 | tf_op jit(solution)/shard_map/all_to_all | solution.py:225
  50.9 0.1 shard_map.41
  51.0 14.1 %all_to_all.22 = f32[144,8,128]{2,1,0:T(8,128)S(1)} all-to-all(f32[144,8,128]{2,1,0:T(8,128)S(1)} %bitcast.7), channel_id=1, replica_groups=mesh['h'=2,'y'=4,'x'=4,'c'=2,'g'=8] {'y','x'}, dimensions={0} | all-to-all | bytes 1179648 | tf_op jit(solution)/shard_map/all_to_all | solution.py:227
  65.0 0.5 shard_map.42
  65.6 25.5 %all_to_all.23.terms_ref = f32[32,4,128]{2,1,0:T(4,128)S(1)} all-to-all(f32[32,4,128]{2,1,0:T(4,128)S(1)} %bitcast.11), channel_id=1, replica_groups=mesh['h'=2,'y'=4,'x'=4,'c'=2,'g'=8] {'h','c','g'}, dimensions={0} | all-to-all | bytes 131072 | tf_op jit(solution)/shard_map/all_to_all | solution.py:229
  91.1 0.9 shard_map.43
Async XLA Ops:
  0.0 11.0 %copy-start = (f32[64,96]{1,0:T(8,128)S(1)}, f32[64,96]{1,0:T(8,128)}, u32[]{:S(2)}) copy-start(f32[64,96]{1,0:T(8,128)} %factor_ref.3) | copy-start | bytes 73732
  2.2 10.7 %collective-permute-start = (f32[4,48,1024]{2,1,0:T(8,128)S(1)}, f32[4,48,1024]{2,1,0:T(8,128)S(1)}, u32[]{:S(2)}, u32[]{:S(2)}) collective-permute-start(f32[4,48,1024]{2,1,0:T(8,128)S(1)} %get-tuple-element.18), channel_id=1, source_target_pairs={{0,8},{8,0},{1,9},{9,1},{2,10},{10,2},{3,11},{11,3},{4,12},{12,4},... | collective-permute-start | bytes 2359304 | tf_op jit(solution)/shard_map/ppermute | solution.py:222
